TPU v7x, 256 devices: a whole 4x4x8 slice. The times are simulated.
256 devices in a mesh: dp: 128 (over x, y_hi, z, core), head: 2 (over y_lo).
Axes of the slice: x: 4, y: 4 (y_hi: 2, y_lo: 2; y = y_hi * 2 + y_lo), z: 8, core: 2. Of those that a mesh axis runs over, the one named last changes fastest.
Arguments:
- picture_tower_summary: bfloat16 [16384, 1536], P('dp'), may hold values from -24 to 24
- caption_tower_summary: bfloat16 [16384, 1536], P('dp'), may hold values from -24 to 24
- picture_head_matrix: bfloat16 [1536, 1536], P(None, 'head'), may hold values from -0.00390625 to 0.00390625
- caption_head_matrix: bfloat16 [1536, 1536], P(None, 'head'), may hold values from -0.00390625 to 0.00390625
- matching_caption_row: int32 [128, 128], P('dp'), may hold values from 0 to 127, each once within a row
- affinity_scale: float32 [1], replicated, may hold values from 4 to 16
- affinity_offset: float32 [1], replicated, may hold values from -4 to -2
Outputs:
- image_loss: float32 [16384], P('dp')
- image_grad_w: float32 [1536, 1536], P('dp', 'head')
- text_grad_w: float32 [1536, 1536], P('dp', 'head')
Inputs may be any that keep to these rules, and one draw needn't show every extreme that they name: Each row of matching_caption_row is a permutation of 0..127.
All inputs are finite; a program needn't handle non-finite values.
Results may differ from a plain program's by a relative error of at most 0.0045.
Values may be sent and summed in bfloat16 or wider, within the bound.
A program may use at most 128 MiB of HBM per device.

v0:
```python
import jax
import jax.numpy as jnp
from jax import lax
from jax.sharding import PartitionSpec as P

REACH = 4


def shifted(value, axis, by):
    peers = lax.axis_size(axis)
    return lax.ppermute(value, axis, [(i, (i + by) % peers) for i in range(peers)])


def embed(features, projection):
    return jnp.dot(features, projection, preferred_element_type=jnp.float32)


def send_home(terms, distance):
    return shifted(terms, "dp", distance)


def shards(
    picture_tower_summary,
    caption_tower_summary,
    picture_head_matrix,
    caption_head_matrix,
    matching_caption_row,
    affinity_scale,
    affinity_offset,
):
    batch_rows = picture_tower_summary.shape[0]
    raw_image = embed(picture_tower_summary, picture_head_matrix)
    raw_text = embed(caption_tower_summary, caption_head_matrix)
    image_sq, text_sq = lax.psum(
        (jnp.sum(raw_image * raw_image, axis=1), jnp.sum(raw_text * raw_text, axis=1)), "head"
    )
    image_inv = lax.rsqrt(image_sq + 1e-06)[:, None]
    text_inv = lax.rsqrt(text_sq + 1e-06)[:, None]
    image_emb = (raw_image * image_inv).astype(jnp.bfloat16)
    text_emb = (raw_text * text_inv).astype(jnp.bfloat16)
    steepness_multiplier = affinity_scale[0]
    shifted_bias = affinity_offset[0]
    positive = (
        lax.broadcasted_iota(jnp.int32, (batch_rows, batch_rows), 1)
        == matching_caption_row[0][:, None]
    ).astype(jnp.float32)
    contract_last = (((1,), (1,)), ((), ()))
    contract_first = (((0,), (0,)), ((), ()))

    def visit(block, labels):
        partial_value = lax.dot_general(
            image_emb, block, contract_last, preferred_element_type=jnp.float32
        )
        pair_logits = steepness_multiplier * lax.psum(partial_value, "head") + shifted_bias
        loss_rows = jnp.sum(jax.nn.softplus(pair_logits) - labels * pair_logits, axis=1)
        logit_slopes = ((jax.nn.sigmoid(pair_logits) - labels) / batch_rows).astype(jnp.bfloat16)
        image_term = steepness_multiplier * jnp.dot(
            logit_slopes, block, preferred_element_type=jnp.float32
        )
        text_term = steepness_multiplier * lax.dot_general(
            logit_slopes, image_emb, contract_first, preferred_element_type=jnp.float32
        )
        return (loss_rows, image_term, text_term)

    loss_sum, image_gradient_sum, text_gradient_sum = visit(text_emb, positive)
    rising = text_emb
    falling = text_emb
    for hop_index in range(1, REACH + 1):
        rising = shifted(rising, "dp", -1)
        falling = shifted(falling, "dp", 1)
        loss_upper, image_upper, text_upper = visit(rising, 0.0)
        loss_lower, image_lower, text_lower = visit(falling, 0.0)
        loss_sum = loss_sum + loss_upper + loss_lower
        image_gradient_sum = image_gradient_sum + image_upper + image_lower
        text_gradient_sum = (
            text_gradient_sum + send_home(text_upper, hop_index) + send_home(text_lower, -hop_index)
        )
    image_wide = image_emb.astype(jnp.float32)
    text_wide = text_emb.astype(jnp.float32)
    image_dot, text_dot = lax.psum(
        (
            jnp.sum(image_wide * image_gradient_sum, axis=1),
            jnp.sum(text_wide * text_gradient_sum, axis=1),
        ),
        "head",
    )
    back_image = ((image_gradient_sum - image_wide * image_dot[:, None]) * image_inv).astype(
        jnp.bfloat16
    )
    back_text = ((text_gradient_sum - text_wide * text_dot[:, None]) * text_inv).astype(
        jnp.bfloat16
    )
    half_width = back_image.shape[1]
    image_part = lax.dot_general(
        picture_tower_summary, back_image, contract_first, preferred_element_type=jnp.float32
    )
    text_part = lax.dot_general(
        caption_tower_summary, back_text, contract_first, preferred_element_type=jnp.float32
    )
    both_grads = lax.psum_scatter(
        jnp.concatenate([image_part, text_part], axis=1), "dp", scatter_dimension=0, tiled=True
    )
    image_loss = loss_sum / batch_rows
    return (image_loss, both_grads[:, :half_width], both_grads[:, half_width:])


def solution(mesh):
    return jax.shard_map(
        shards,
        mesh=mesh,
        in_specs=(
            P("dp", None),
            P("dp", None),
            P(None, "head"),
            P(None, "head"),
            P("dp", None),
            P(),
            P(),
        ),
        out_specs=(P("dp"), P("dp", "head"), P("dp", "head")),
        check_vma=False,
    )
```

profile of v0, /device:TPU:1, one launch (start us, length us, event | category | flops | bytes accessed | tf_op | source)
XLA Modules:
  0.0 1481.5 jit_solution(17595157580005823079)
XLA Ops:
  7.2 1.6 copy-done
  8.8 1.6 multiply_reduce_fusion.1
  10.4 2.4 multiply_reduce_fusion
  12.8 4.4 all-reduce.2
  17.3 3.6 collective-permute-start.1
  22.2 1.4 collective-permute-done.1
  23.5 2.5 collective-permute-start.3
  26.9 5.9 collective-permute-start.2
  34.5 9.1 collective-permute-start.4
  45.3 9.1 collective-permute-start.6
  59.0 48.7 %all-reduce.9.cloned.1.call-done = (f32[128,128]{1,0:T(8,128)}, f32[128,128]{1,0:T(8,128)}, f32[128,128]{1,0:T(8,128)}, f32[128,128]{1,0:T(8,128)}, f32[128,128]...) async-done(((f32[128,128]{1,0:T(8,128)}, f32[128,128]{1,0:T(8,128)}, f32[128,128]{1,0:T(8,128)}, ...) | async-done | bytes 589840 | tf_op jit(solution)/shard_map/psum | solution.py:54
  107.8 1.2 convolution_multiply_fusion
  108.9 8.2 collective-permute-start.15
  117.1 1.1 convolution_multiply_fusion.1
  118.4 1.1 convolution_multiply_fusion.2
  119.5 8.4 collective-permute-start.13
  128.0 1.1 convolution_multiply_fusion.3
  129.2 1.1 convolution_multiply_fusion.4
  130.3 7.5 collective-permute-start.11
  137.8 1.1 convolution_multiply_fusion.5
  139.0 1.1 convolution_multiply_fusion.6
  140.1 1.1 convolution_multiply_fusion.7
  143.6 4.8 collective-permute-start.9
  148.9 8.1 collective-permute-done.12
  157.0 6.8 collective-permute-done.10
  163.9 1.7 fusion.16
  165.5 4.5 all-reduce.1
  170.0 1.9 convolution_bitcast_fusion
  172.0 3.1 convolution_bitcast_fusion.1
  175.1 6.8 pad_maximum_fusion
  185.3 1286.2 %all-reduce.7.cloned.1.call-done = f32[1536,1536]{0,1:T(8,128)} async-done(((f32[1536,1536]{0,1:T(8,128)}), f32[1536,1536]{0,1:T(8,128)}) %all-reduce.7.cloned.1.call-update) | async-done | bytes 9437200
  1471.5 1.6 fusion.48
  (118 shorter events, 16.0 us)
Async XLA Ops:
  7.2 100.6 %all-reduce.9.cloned.1.call-start = ((), (), s32[]{:S(2)}) async-start(), calls=%async_computation.1 | async-start | bytes 1179648 | tf_op jit(solution)/shard_map/psum | solution.py:54
  17.3 6.2 collective-permute-start.1
  20.9 5.9 collective-permute-start
  22.2 119.0 %copy-start.29 = (s32[1,128]{1,0:T(1,128)S(1)}, s32[1,128]{1,0:T(1,128)}, u32[]{:S(2)}) copy-start(s32[1,128]{1,0:T(1,128)} %param.11) | copy-start | bytes 1540
  23.5 10.1 collective-permute-start.3
  26.9 7.6 collective-permute-start.2
  33.6 10.8 collective-permute-start.5
  34.5 10.8 collective-permute-start.4
  44.5 11.7 copy-start.9
  44.5 10.8 collective-permute-start.7
  45.3 10.8 collective-permute-start.6
  57.7 1413.8 %all-reduce.7.cloned.1.call-start = ((), (), s32[]{:S(2)}) async-start(), calls=%async_computation | async-start | bytes 18874368
  107.8 33.4 %copy-start.11 = (f32[128,128]{1,0:T(8,128)S(1)}, f32[128,128]{1,0:T(8,128)}, u32[]{:S(2)}) copy-start(f32[128,128]{1,0:T(8,128)} %get-tuple-element.20) | copy-start | bytes 196612
  107.8 33.7 %copy-start.8 = (bf16[128,768]{1,0:T(8,128)(2,1)S(1)}, bf16[128,768]{1,0:T(8,128)(2,1)}, u32[]{:S(2)}) copy-start(bf16[128,768]{1,0:T(8,128)(2,1)} %copy-done.7) | copy-start | bytes 589828
  107.8 33.7 %copy-start.21 = (f32[128,128]{1,0:T(8,128)S(1)}, f32[128,128]{1,0:T(8,128)}, u32[]{:S(2)}) copy-start(f32[128,128]{1,0:T(8,128)} %get-tuple-element.17) | copy-start | bytes 196612
  107.8 33.9 %copy-start.13 = (f32[128,128]{1,0:T(8,128)S(1)}, f32[128,128]{1,0:T(8,128)}, u32[]{:S(2)}) copy-start(f32[128,128]{1,0:T(8,128)} %get-tuple-element.21) | copy-start | bytes 196612
  107.8 34.1 %copy-start.17 = (f32[128,128]{1,0:T(8,128)S(1)}, f32[128,128]{1,0:T(8,128)}, u32[]{:S(2)}) copy-start(f32[128,128]{1,0:T(8,128)} %get-tuple-element.19) | copy-start | bytes 196612
  107.8 34.3 %copy-start.15 = (f32[128,128]{1,0:T(8,128)S(1)}, f32[128,128]{1,0:T(8,128)}, u32[]{:S(2)}) copy-start(f32[128,128]{1,0:T(8,128)} %get-tuple-element.18) | copy-start | bytes 196612
  108.9 33.9 %collective-permute-start.15 = (f32[128,768]{1,0:T(8,128)S(1)}, f32[128,768]{1,0:T(8,128)S(1)}, u32[]{:S(2)}, u32[]{:S(2)}) collective-permute-start(f32[128,768]{1,0:T(8,128)S(1)} %convolution_multiply_fusion), channel_id=1, source_target_pairs={{0,248},{2,250},{4,252},{6,254},{8,0},{10,2},{12,4},{14,6},{16,8},... | collective-permute-start | bytes 1179656 | tf_op jit(solution)/shard_map/ppermute | solution.py:11
  117.1 25.2 %copy-start.10 = (bf16[128,768]{1,0:T(8,128)(2,1)S(1)}, bf16[128,768]{1,0:T(8,128)(2,1)}, u32[]{:S(2)}) copy-start(bf16[128,768]{1,0:T(8,128)(2,1)} %copy-done.9) | copy-start | bytes 589828
  117.1 25.2 %copy-start.25 = (f32[128,128]{1,0:T(8,128)S(1)}, f32[128,128]{1,0:T(8,128)}, u32[]{:S(2)}) copy-start(f32[128,128]{1,0:T(8,128)} %get-tuple-element.15) | copy-start | bytes 196612
  118.3 25.3 %collective-permute-start.14 = (f32[128,768]{1,0:T(8,128)S(1)}, f32[128,768]{1,0:T(8,128)S(1)}, u32[]{:S(2)}, u32[]{:S(2)}) collective-permute-start(f32[128,768]{1,0:T(8,128)S(1)} %convolution_multiply_fusion.1), channel_id=1, source_target_pairs={{0,8},{2,10},{4,12},{6,14},{8,16},{10,18},{12,20},{14,22},{16,24},... | collective-permute-start | bytes 1179656 | tf_op jit(solution)/shard_map/ppermute | solution.py:11
  118.4 24.2 %copy-start.19 = (f32[128,128]{1,0:T(8,128)S(1)}, f32[128,128]{1,0:T(8,128)}, u32[]{:S(2)}) copy-start(f32[128,128]{1,0:T(8,128)} %get-tuple-element.16) | copy-start | bytes 196612
  119.5 28.9 %collective-permute-start.13 = (f32[128,768]{1,0:T(8,128)S(1)}, f32[128,768]{1,0:T(8,128)S(1)}, u32[]{:S(2)}, u32[]{:S(2)}) collective-permute-start(f32[128,768]{1,0:T(8,128)S(1)} %convolution_multiply_fusion.2), channel_id=1, source_target_pairs={{0,250},{2,252},{4,254},{6,0},{8,2},{10,4},{12,6},{14,8},{16,10},{... | collective-permute-start | bytes 1179656 | tf_op jit(solution)/shard_map/ppermute | solution.py:11
  129.1 28.0 %collective-permute-start.12 = (f32[128,768]{1,0:T(8,128)S(1)}, f32[128,768]{1,0:T(8,128)S(1)}, u32[]{:S(2)}, u32[]{:S(2)}) collective-permute-start(f32[128,768]{1,0:T(8,128)S(1)} %convolution_multiply_fusion.3), channel_id=1, source_target_pairs={{0,6},{2,8},{4,10},{6,12},{8,14},{10,16},{12,18},{14,20},{16,22},{... | collective-permute-start | bytes 1179656 | tf_op jit(solution)/shard_map/ppermute | solution.py:11
  129.2 19.2 %copy-start.6 = (bf16[128,768]{1,0:T(8,128)(2,1)S(1)}, bf16[128,768]{1,0:T(8,128)(2,1)}, u32[]{:S(2)}) copy-start(bf16[128,768]{1,0:T(8,128)(2,1)} %copy-done.5) | copy-start | bytes 589828
  129.2 19.2 %copy-start.27 = (f32[128,128]{1,0:T(8,128)S(1)}, f32[128,128]{1,0:T(8,128)}, u32[]{:S(2)}) copy-start(f32[128,128]{1,0:T(8,128)} %get-tuple-element.13) | copy-start | bytes 196612
  130.3 26.7 %collective-permute-start.11 = (f32[128,768]{1,0:T(8,128)S(1)}, f32[128,768]{1,0:T(8,128)S(1)}, u32[]{:S(2)}, u32[]{:S(2)}) collective-permute-start(f32[128,768]{1,0:T(8,128)S(1)} %convolution_multiply_fusion.4), channel_id=1, source_target_pairs={{0,252},{2,254},{4,0},{6,2},{8,4},{10,6},{12,8},{14,10},{16,12},{1... | collective-permute-start | bytes 1179656 | tf_op jit(solution)/shard_map/ppermute | solution.py:11
  142.1 27.9 %copy-start.1 = (bf16[128,1536]{1,0:T(8,128)(2,1)S(1)}, bf16[128,1536]{1,0:T(8,128)(2,1)}, u32[]{:S(2)}) copy-start(bf16[128,1536]{1,0:T(8,128)(2,1)} %param.8) | copy-start | bytes 1179652
  142.8 21.0 %collective-permute-start.10 = (f32[128,768]{1,0:T(8,128)S(1)}, f32[128,768]{1,0:T(8,128)S(1)}, u32[]{:S(2)}, u32[]{:S(2)}) collective-permute-start(f32[128,768]{1,0:T(8,128)S(1)} %convolution_multiply_fusion.5), channel_id=1, source_target_pairs={{0,4},{2,6},{4,8},{6,10},{8,12},{10,14},{12,16},{14,18},{16,20},{1... | collective-permute-start | bytes 1179656 | tf_op jit(solution)/shard_map/ppermute | solution.py:11
  143.6 20.2 %collective-permute-start.9 = (f32[128,768]{1,0:T(8,128)S(1)}, f32[128,768]{1,0:T(8,128)S(1)}, u32[]{:S(2)}, u32[]{:S(2)}) collective-permute-start(f32[128,768]{1,0:T(8,128)S(1)} %convolution_multiply_fusion.6), channel_id=1, source_target_pairs={{0,254},{2,0},{4,2},{6,4},{8,6},{10,8},{12,10},{14,12},{16,14},{18... | collective-permute-start | bytes 1179656 | tf_op jit(solution)/shard_map/ppermute | solution.py:11
  148.4 15.5 %collective-permute-start.8 = (f32[128,768]{1,0:T(8,128)S(1)}, f32[128,768]{1,0:T(8,128)S(1)}, u32[]{:S(2)}, u32[]{:S(2)}) collective-permute-start(f32[128,768]{1,0:T(8,128)S(1)} %convolution_multiply_fusion.7), channel_id=1, source_target_pairs={{0,2},{2,4},{4,6},{6,8},{8,10},{10,12},{12,14},{14,16},{16,18},{18... | collective-permute-start | bytes 1179656 | tf_op jit(solution)/shard_map/ppermute | solution.py:11
  (18 other events, 61.6 us)
Sparse Core Ops, SparseCore 0:
  57.8 49.8 all-reduce.8
  182.2 1289.2 all-reduce.6
where the time goes:
time: 1490 us; the launch traced here: 1480 us
  waiting for transfers between devices  1350 us (91%)
  starting transfers between devices  59.8 us (4%)
  matrix products  29.2 us (2%)
  between operations  16.5 us (1%)
    unnamed x3, waiting for transfers between devices  1290 us
    ppermute x16, starting transfers between devices, shifted(): lax.ppermute(value, axis, [(i, (i + by) % peers) for i in range(peers)])  59.7 us
    psum x1, waiting for transfers between devices, visit(): lax.psum(partial_value, 'head')  48.7 us
  transfers between devices with their start and end apart: 18, of which 6 were waited for; matrix products, arithmetic and copies ran while one was open for 1% of the time, Pallas kernels for 0%

commit v1 on v0

--- a/solution.py
+++ b/solution.py
@@ -1,9 +1,173 @@
+import functools
+
 import jax
 import jax.numpy as jnp
+import numpy as np
 from jax import lax
+from jax.experimental import pallas as pl
+from jax.experimental.pallas import tpu as pltpu
 from jax.sharding import PartitionSpec as P
 
+MESH = pl.DeviceIdType.MESH
 REACH = 4
+XS, YS, ZS = 4, 2, 8
+GROUP = 2 * YS
+
+
+def column_order():
+    order = np.arange(XS * YS * ZS * 2 * 12).reshape(XS, YS, ZS, 2, 12)
+    return order.transpose(1, 3, 0, 2, 4).reshape(1, -1).astype(np.int32)
+
+
+def weight_kernel(
+    picture_ref, caption_ref, image_ref, text_ref, order_ref, image_out, text_out,
+    towers_out, towers, backs, total, x_out, x_in, z_own, z_out, z_in, send, recv,
+):
+    dp, side = lax.axis_index("dp"), lax.axis_index("head")
+    core = lax.rem(dp, 2)
+    z = lax.rem(lax.div(dp, 2), ZS)
+    y = lax.rem(lax.div(dp, 2 * ZS), YS)
+    x = lax.div(dp, 2 * ZS * YS)
+
+    def place(x, y, z, core):
+        return ((x * YS + y) * ZS + z) * 2 + core
+
+    sibling = (place(x, y, z, 1 - core), side)
+    over = (place(x, 1 - y, z, core), side)
+    crossed = [(place(x, 1 - y, z, c), 1 - side) for c in range(2)]
+    x_peers = [(place(lax.rem(x + d, XS), y, z, core), side) for d in range(1, XS)]
+    z_peers = [(place(x, y, lax.rem(z + d, ZS), core), side) for d in range(1, ZS)]
+    greeted = [sibling, over, *crossed, *x_peers, *z_peers]
+    barrier = pltpu.get_barrier_semaphore()
+    for peer in greeted:
+        pl.semaphore_signal(barrier, inc=1, device_id=peer, device_id_type=MESH)
+
+    mine = y * 2 + core
+    columns = order_ref.shape[1]
+    part = columns // GROUP
+    rows = picture_ref.shape[0]
+    pair = jnp.concatenate([picture_ref[...], caption_ref[...]], axis=0)
+    wide = columns // XS
+    for g in range(GROUP):
+        pick = order_ref[:, g * part : (g + 1) * part]
+        acc = None
+        for b in range(XS):
+            chosen = (lax.broadcasted_iota(jnp.int32, (wide, part), 0) + b * wide == pick)
+            one = jnp.where(chosen, 1.0, 0.0).astype(jnp.bfloat16)
+            term = jnp.dot(pair[:, b * wide : (b + 1) * wide], one, preferred_element_type=jnp.float32)
+            acc = term if acc is None else acc + term
+        towers_out[g, 0] = acc[:rows].astype(jnp.bfloat16)
+        towers_out[g, 1] = acc[rows:].astype(jnp.bfloat16)
+    towers[mine] = towers_out[mine]
+    backs[0, mine] = image_ref[...]
+    backs[1, mine] = text_ref[...]
+
+    pl.semaphore_wait(barrier, len(greeted))
+
+    used = [0]
+
+    def copy(src, dst, peer, arrival=None):
+        at = used[0]
+        used[0] += 1
+        made = pltpu.make_async_remote_copy(
+            src_ref=src, dst_ref=dst, send_sem=send.at[at],
+            recv_sem=recv.at[at if arrival is None else arrival],
+            device_id=peer, device_id_type=MESH,
+        )
+        made.start()
+        return made
+
+    def landed(dst, arrival):
+        pltpu.make_async_copy(dst, dst, recv.at[arrival]).wait()
+
+    cross_slot = (1 - y) * 2
+    first = []
+    for t in range(2):
+        first.append((
+            copy(backs.at[t, mine], backs.at[t, mine], over),
+            copy(backs.at[t, mine], backs.at[t, mine], sibling),
+        ))
+    moved = [copy(towers_out.at[y * 2 + 1 - core], towers.at[mine], sibling)]
+    base = used[0]
+    for c in range(2):
+        moved.append(copy(towers_out.at[cross_slot + c], towers.at[mine], crossed[c], base + core))
+    passed = []
+    for t in range(2):
+        first[t][0].wait_recv()
+        far = cross_slot + core
+        passed.append(copy(backs.at[t, far], backs.at[t, far], sibling))
+    moved[0].wait_recv()
+    for c in range(2):
+        landed(towers.at[cross_slot + c], base + c)
+    spread = []
+    for t in range(2):
+        first[t][1].wait_recv()
+        passed[t].wait_recv()
+        left = towers[:, t].reshape(GROUP * rows, part)
+        right = backs[t].reshape(GROUP * rows, backs.shape[3])
+        product = lax.dot_general(left, right, (((0,), (0,)), ((), ())), preferred_element_type=jnp.float32)
+        product = product.reshape(XS, part // XS, backs.shape[3])
+        total[t] = product
+        x_out[t] = product.astype(jnp.bfloat16)
+        row = []
+        for d in range(1, XS):
+            row.append(copy(x_out.at[t, lax.rem(x + d, XS)], x_in.at[t, d - 1], x_peers[d - 1]))
+        spread.append(row)
+    last = []
+    for t in range(2):
+        value = total[t, x]
+        for d in range(XS - 1):
+            spread[t][d].wait_recv()
+            value = value + x_in[t, d].astype(jnp.float32)
+        for c in range(ZS):
+            chunk = value[c * 12 : (c + 1) * 12]
+            chunk = jnp.concatenate([chunk, jnp.zeros((4, chunk.shape[1]), jnp.float32)], axis=0)
+            z_own[t, c] = chunk
+            z_out[t, c] = chunk.astype(jnp.bfloat16)
+        row = []
+        for d in range(1, ZS):
+            row.append(copy(z_out.at[t, lax.rem(z + d, ZS)], z_in.at[t, d - 1], z_peers[d - 1]))
+        last.append(row)
+    for t, out in ((0, image_out), (1, text_out)):
+        value = z_own[t, z]
+        for d in range(ZS - 1):
+            last[t][d].wait_recv()
+            value = value + z_in[t, d].astype(jnp.float32)
+        out[...] = value[:12]
+    for group in (*first, moved, passed, *spread, *last):
+        for m in group:
+            m.wait_send()
+
+
+def weight_grads(picture, caption, back_image, back_text):
+    rows, columns = picture.shape
+    half = back_image.shape[1]
+    part = columns // GROUP
+    bf, f32 = jnp.bfloat16, jnp.float32
+    copies = 4 + 3 + 2 + 2 * (XS - 1) + 2 * (ZS - 1)
+    vmem = pl.BlockSpec(memory_space=pltpu.VMEM)
+    return pl.pallas_call(
+        weight_kernel,
+        out_shape=[jax.ShapeDtypeStruct((12, half), f32)] * 2,
+        in_specs=[vmem] * 5,
+        out_specs=[vmem] * 2,
+        scratch_shapes=[
+            pltpu.VMEM((GROUP, 2, rows, part), bf),
+            pltpu.VMEM((GROUP, 2, rows, part), bf),
+            pltpu.VMEM((2, GROUP, rows, half), bf),
+            pltpu.VMEM((2, XS, part // XS, half), f32),
+            pltpu.VMEM((2, XS, part // XS, half), bf),
+            pltpu.VMEM((2, XS - 1, part // XS, half), bf),
+            pltpu.VMEM((2, ZS, 16, half), f32),
+            pltpu.VMEM((2, ZS, 16, half), bf),
+            pltpu.VMEM((2, ZS - 1, 16, half), bf),
+            pltpu.SemaphoreType.DMA((copies,)),
+            pltpu.SemaphoreType.DMA((copies,)),
+        ],
+        compiler_params=pltpu.CompilerParams(
+            collective_id=0, has_side_effects=True, vmem_limit_bytes=48 * 1024 * 1024
+        ),
+    )(picture, caption, back_image, back_text, jnp.asarray(column_order()))
 
 
 def shifted(value, axis, by):
@@ -90,18 +254,11 @@
     back_text = ((text_gradient_sum - text_wide * text_dot[:, None]) * text_inv).astype(
         jnp.bfloat16
     )
-    half_width = back_image.shape[1]
-    image_part = lax.dot_general(
-        picture_tower_summary, back_image, contract_first, preferred_element_type=jnp.float32
-    )
-    text_part = lax.dot_general(
-        caption_tower_summary, back_text, contract_first, preferred_element_type=jnp.float32
-    )
-    both_grads = lax.psum_scatter(
-        jnp.concatenate([image_part, text_part], axis=1), "dp", scatter_dimension=0, tiled=True
+    image_grad_w, text_grad_w = weight_grads(
+        picture_tower_summary, caption_tower_summary, back_image, back_text
     )
     image_loss = loss_sum / batch_rows
-    return (image_loss, both_grads[:, :half_width], both_grads[:, half_width:])
+    return (image_loss, image_grad_w, text_grad_w)
 
 
 def solution(mesh):

time: 1490 us -> 220 us (0.15)
  waiting for transfers between devices: 1350 us -> 66.7 us
  Pallas kernels: 0 us -> 41.5 us
    unnamed x3 -> x1, waiting for transfers between devices: 1290 us -> 0.02 us
    pallas_call x0 -> x1, Pallas kernels: none -> 41.5 us  [weight_grads(): pl.pallas_call(weight_kernel, out_shape=[jax.ShapeDtypeStruct((12, half),...]
  transfers between devices with their start and end apart: 18 -> 17, of which waited for: 6 -> 5; matrix products, arithmetic and copies ran while one was open for 1% -> 7% of each run, Pallas kernels for 0% -> 0%
where the time goes in v1:
time: 220 us
  waiting for transfers between devices  66.7 us (30%)
  starting transfers between devices  59.7 us (27%)
  Pallas kernels  41.5 us (19%)
  matrix products  20.9 us (10%)
  between operations  15.8 us (7%)
  blocking collectives  8.31 us (4%)
  other arithmetic  4.08 us (2%)
  local copies, waits for them, and re-layouts  3.03 us (1%)
    ppermute x16, starting transfers between devices, shifted(): lax.ppermute(value, axis, [(i, (i + by) % peers) for i in range(peers)])  59.7 us
    psum x1, waiting for transfers between devices, visit(): lax.psum(partial_value, 'head')  48.8 us
    pallas_call x1, Pallas kernels, weight_grads(): pl.pallas_call(weight_kernel, out_shape=[jax.ShapeDtypeStruct((12, half),...  41.5 us
    ppermute x16, waiting for transfers between devices, shifted(): lax.ppermute(value, axis, [(i, (i + by) % peers) for i in range(peers)])  17.9 us
    dot_general x9, matrix products, visit(): lax.dot_general(image_emb, block, contract_last, preferred_element_type=j...  7.53 us
    dot_general x9, matrix products, visit(): lax.dot_general(logit_slopes, image_emb, contract_first, preferred_elemen...  7.16 us
    psum x1, blocking collectives, shards(): lax.psum((jnp.sum(raw_image * raw_image, axis=1), jnp.sum(raw_text * raw_...  4.41 us
  transfers between devices with their start and end apart: 17, of which 5 were waited for; matrix products, arithmetic and copies ran while one was open for 7% of the time, Pallas kernels for 0%

profile of v1, /device:TPU:1, one launch (start us, length us, event | category | flops | bytes accessed | tf_op | source)
XLA Modules:
  0.0 219.9 jit_solution(16904588371173820135)
XLA Ops:
  7.2 1.6 copy-done
  8.8 1.7 multiply_reduce_fusion.1
  10.6 1.2 multiply_reduce_fusion
  11.9 4.4 %all-reduce.1 = (f32[128]{0:T(128)S(1)}, f32[128]{0:T(128)S(1)}) all-reduce(f32[128]{0:T(128)S(1)} %get-tuple-element.20, f32[128]{0:T(128)S(1)} %get-tuple-element.22), channel_id=1, replica_groups=mesh['dp'=128,'head'=2] {'head'}, use_global_device_ids=true, to_apply=%region_1.0 | all-reduce | flops 256 | bytes 2048 | tf_op jit(solution)/shard_map/psum | solution.py:198
  16.3 1.1 multiply_convert_fusion
  17.4 3.6 %collective-permute-start.1 = (bf16[128,768]{1,0:T(8,128)(2,1)S(1)}, bf16[128,768]{1,0:T(8,128)(2,1)S(1)}, u32[]{:S(2)}, u32[]{:S(2)}) collective-permute-start(bf16[128,768]{1,0:T(8,128)(2,1)S(1)} %multiply_convert_fusion), channel_id=1, source_target_pairs={{0,2},{2,4},{4,6},{6,8},{8,10},{10,12},{12,14},{14,16},{16,18},{18... | collective-permute-start | bytes 589832 | tf_op jit(solution)/shard_map/ppermute | solution.py:175
  22.2 1.4 collective-permute-done.1
  23.6 2.5 %collective-permute-start.3 = (bf16[128,768]{1,0:T(8,128)(2,1)S(1)}, bf16[128,768]{1,0:T(8,128)(2,1)S(1)}, u32[]{:S(2)}, u32[]{:S(2)}) collective-permute-start(bf16[128,768]{1,0:T(8,128)(2,1)S(1)} %collective-permute-done.1), channel_id=1, source_target_pairs={{0,2},{2,4},{4,6},{6,8},{8,10},{10,12},{12,14},{14,16},{16,18},{18... | collective-permute-start | bytes 589832 | tf_op jit(solution)/shard_map/ppermute | solution.py:175
  26.1 0.8 fusion.44
  26.9 5.9 %collective-permute-start.2 = (bf16[128,768]{1,0:T(8,128)(2,1)S(1)}, bf16[128,768]{1,0:T(8,128)(2,1)S(1)}, u32[]{:S(2)}, u32[]{:S(2)}) collective-permute-start(bf16[128,768]{1,0:T(8,128)(2,1)S(1)} %collective-permute-done), channel_id=1, source_target_pairs={{0,254},{2,0},{4,2},{6,4},{8,6},{10,8},{12,10},{14,12},{16,14},{18... | collective-permute-start | bytes 589832 | tf_op jit(solution)/shard_map/ppermute | solution.py:175
  32.9 0.8 fusion.43
  33.7 0.8 fusion.46
  34.6 9.1 %collective-permute-start.4 = (bf16[128,768]{1,0:T(8,128)(2,1)S(1)}, bf16[128,768]{1,0:T(8,128)(2,1)S(1)}, u32[]{:S(2)}, u32[]{:S(2)}) collective-permute-start(bf16[128,768]{1,0:T(8,128)(2,1)S(1)} %collective-permute-done.2), channel_id=1, source_target_pairs={{0,254},{2,0},{4,2},{6,4},{8,6},{10,8},{12,10},{14,12},{16,14},{18... | collective-permute-start | bytes 589832 | tf_op jit(solution)/shard_map/ppermute | solution.py:175
  44.5 0.8 fusion.48
  45.4 9.1 %collective-permute-start.6 = (bf16[128,768]{1,0:T(8,128)(2,1)S(1)}, bf16[128,768]{1,0:T(8,128)(2,1)S(1)}, u32[]{:S(2)}, u32[]{:S(2)}) collective-permute-start(bf16[128,768]{1,0:T(8,128)(2,1)S(1)} %collective-permute-done.4), channel_id=1, source_target_pairs={{0,254},{2,0},{4,2},{6,4},{8,6},{10,8},{12,10},{14,12},{16,14},{18... | collective-permute-start | bytes 589832 | tf_op jit(solution)/shard_map/ppermute | solution.py:175
  58.4 48.8 %all-reduce.5.cloned.1.call-done = (f32[128,128]{1,0:T(8,128)}, f32[128,128]{1,0:T(8,128)}, f32[128,128]{1,0:T(8,128)}, f32[128,128]{1,0:T(8,128)}, f32[128,128]...) async-done(((f32[128,128]{1,0:T(8,128)}, f32[128,128]{1,0:T(8,128)}, f32[128,128]{1,0:T(8,128)}, ...) | async-done | bytes 589840 | tf_op jit(solution)/shard_map/psum | solution.py:218
  107.2 1.1 convolution_multiply_fusion
  108.3 8.2 %collective-permute-start.15 = (f32[128,768]{1,0:T(8,128)S(1)}, f32[128,768]{1,0:T(8,128)S(1)}, u32[]{:S(2)}, u32[]{:S(2)}) collective-permute-start(f32[128,768]{1,0:T(8,128)S(1)} %convolution_multiply_fusion), channel_id=1, source_target_pairs={{0,248},{2,250},{4,252},{6,254},{8,0},{10,2},{12,4},{14,6},{16,8},... | collective-permute-start | bytes 1179656 | tf_op jit(solution)/shard_map/ppermute | solution.py:175
  116.5 1.1 convolution_multiply_fusion.1
  117.8 1.1 convolution_multiply_fusion.2
  118.9 8.4 %collective-permute-start.13 = (f32[128,768]{1,0:T(8,128)S(1)}, f32[128,768]{1,0:T(8,128)S(1)}, u32[]{:S(2)}, u32[]{:S(2)}) collective-permute-start(f32[128,768]{1,0:T(8,128)S(1)} %convolution_multiply_fusion.2), channel_id=1, source_target_pairs={{0,250},{2,252},{4,254},{6,0},{8,2},{10,4},{12,6},{14,8},{16,10},{... | collective-permute-start | bytes 1179656 | tf_op jit(solution)/shard_map/ppermute | solution.py:175
  127.3 1.1 convolution_multiply_fusion.3
  128.8 7.5 %collective-permute-start.11 = (f32[128,768]{1,0:T(8,128)S(1)}, f32[128,768]{1,0:T(8,128)S(1)}, u32[]{:S(2)}, u32[]{:S(2)}) collective-permute-start(f32[128,768]{1,0:T(8,128)S(1)} %convolution_multiply_fusion.4), channel_id=1, source_target_pairs={{0,252},{2,254},{4,0},{6,2},{8,4},{10,6},{12,8},{14,10},{16,12},{1... | collective-permute-start | bytes 1179656 | tf_op jit(solution)/shard_map/ppermute | solution.py:175
  139.9 3.1 %collective-permute-done.14 = f32[128,768]{1,0:T(8,128)S(1)} collective-permute-done((f32[128,768]{1,0:T(8,128)S(1)}, f32[128,768]{1,0:T(8,128)S(1)}, u32[]{:S(2)}, u32[]{:S(2)}) %collective-permute-start.14) | collective-permute-done | bytes 393248 | tf_op jit(solution)/shard_map/ppermute | solution.py:175
  143.1 4.7 %collective-permute-start.9 = (f32[128,768]{1,0:T(8,128)S(1)}, f32[128,768]{1,0:T(8,128)S(1)}, u32[]{:S(2)}, u32[]{:S(2)}) collective-permute-start(f32[128,768]{1,0:T(8,128)S(1)} %convolution_multiply_fusion.6), channel_id=1, source_target_pairs={{0,254},{2,0},{4,2},{6,4},{8,6},{10,8},{12,10},{14,12},{16,14},{18... | collective-permute-start | bytes 1179656 | tf_op jit(solution)/shard_map/ppermute | solution.py:175
  148.3 1.6 fusion.12
  149.9 6.6 %collective-permute-done.12 = f32[128,768]{1,0:T(8,128)S(1)} collective-permute-done((f32[128,768]{1,0:T(8,128)S(1)}, f32[128,768]{1,0:T(8,128)S(1)}, u32[]{:S(2)}, u32[]{:S(2)}) %collective-permute-start.12) | collective-permute-done | bytes 393248 | tf_op jit(solution)/shard_map/ppermute | solution.py:175
  156.4 6.8 %collective-permute-done.10 = f32[128,768]{1,0:T(8,128)S(1)} collective-permute-done((f32[128,768]{1,0:T(8,128)S(1)}, f32[128,768]{1,0:T(8,128)S(1)}, u32[]{:S(2)}, u32[]{:S(2)}) %collective-permute-start.10) | collective-permute-done | bytes 393248 | tf_op jit(solution)/shard_map/ppermute | solution.py:175
  163.2 1.7 fusion.16
  164.9 3.9 %all-reduce = (f32[128]{0:T(128)S(1)}, f32[128]{0:T(128)S(1)}) all-reduce(f32[128]{0:T(128)} %get-tuple-element.24, f32[128]{0:T(128)} %get-tuple-element.26), channel_id=1, replica_groups=mesh['dp'=128,'head'=2] {'head'}, use_global_device_ids=true, to_apply=%region_23.24 | all-reduce | flops 256 | bytes 2048 | tf_op jit(solution)/shard_map/psum | solution.py:244
  168.8 1.5 fusion.15
  170.4 41.5 %shard_map.103 = (f32[12,768]{1,0:T(8,128)S(1)}, f32[12,768]{1,0:T(8,128)S(1)}) custom-call(bf16[128,1536]{1,0:T(8,128)(2,1)S(1)} %copy-done.1, bf16[128,1536]{1,0:T(8,128)(2,1)S(1)} %copy-done.2, bf16[128,768]{1,0:T(8,128)(2,1)S(1)} %get-tuple-element.36.image_ref, bf16[128,768]{1,0:T(8,128)(2,1)S(1)} %get-tuple-element.37.text_ref, s32[1,1536]{1,0:T(1,128)S(1)} %copy-done.3), custom_call_target="tpu_custom_call" | custom-call | tf_op jit(solution)/shard_map/pallas_call | solution.py:149
  (104 shorter events, 10.4 us)
Async XLA Ops:
  7.2 100.0 %all-reduce.5.cloned.1.call-start = ((), (), s32[]{:S(2)}) async-start(), calls=%async_computation | async-start | bytes 1179648 | tf_op jit(solution)/shard_map/psum | solution.py:218
  17.4 6.2 %collective-permute-start.1 = (bf16[128,768]{1,0:T(8,128)(2,1)S(1)}, bf16[128,768]{1,0:T(8,128)(2,1)S(1)}, u32[]{:S(2)}, u32[]{:S(2)}) collective-permute-start(bf16[128,768]{1,0:T(8,128)(2,1)S(1)} %multiply_convert_fusion), channel_id=1, source_target_pairs={{0,2},{2,4},{4,6},{6,8},{8,10},{10,12},{12,14},{14,16},{16,18},{18... | collective-permute-start | bytes 589832 | tf_op jit(solution)/shard_map/ppermute | solution.py:175
  21.0 5.9 %collective-permute-start = (bf16[128,768]{1,0:T(8,128)(2,1)S(1)}, bf16[128,768]{1,0:T(8,128)(2,1)S(1)}, u32[]{:S(2)}, u32[]{:S(2)}) collective-permute-start(bf16[128,768]{1,0:T(8,128)(2,1)S(1)} %multiply_convert_fusion), channel_id=1, source_target_pairs={{0,254},{2,0},{4,2},{6,4},{8,6},{10,8},{12,10},{14,12},{16,14},{18... | collective-permute-start | bytes 589832 | tf_op jit(solution)/shard_map/ppermute | solution.py:175
  23.6 32.6 %copy-start.6 = (bf16[128,768]{1,0:T(8,128)(2,1)}, bf16[128,768]{1,0:T(8,128)(2,1)S(1)}, u32[]{:S(2)}) copy-start(bf16[128,768]{1,0:T(8,128)(2,1)S(1)} %collective-permute-done.1) | copy-start | bytes 589828
  23.6 10.1 %collective-permute-start.3 = (bf16[128,768]{1,0:T(8,128)(2,1)S(1)}, bf16[128,768]{1,0:T(8,128)(2,1)S(1)}, u32[]{:S(2)}, u32[]{:S(2)}) collective-permute-start(bf16[128,768]{1,0:T(8,128)(2,1)S(1)} %collective-permute-done.1), channel_id=1, source_target_pairs={{0,2},{2,4},{4,6},{6,8},{8,10},{10,12},{12,14},{14,16},{16,18},{18... | collective-permute-start | bytes 589832 | tf_op jit(solution)/shard_map/ppermute | solution.py:175
  26.9 29.3 %copy-start.8 = (bf16[128,768]{1,0:T(8,128)(2,1)}, bf16[128,768]{1,0:T(8,128)(2,1)S(1)}, u32[]{:S(2)}) copy-start(bf16[128,768]{1,0:T(8,128)(2,1)S(1)} %collective-permute-done) | copy-start | bytes 589828
  26.9 7.6 %collective-permute-start.2 = (bf16[128,768]{1,0:T(8,128)(2,1)S(1)}, bf16[128,768]{1,0:T(8,128)(2,1)S(1)}, u32[]{:S(2)}, u32[]{:S(2)}) collective-permute-start(bf16[128,768]{1,0:T(8,128)(2,1)S(1)} %collective-permute-done), channel_id=1, source_target_pairs={{0,254},{2,0},{4,2},{6,4},{8,6},{10,8},{12,10},{14,12},{16,14},{18... | collective-permute-start | bytes 589832 | tf_op jit(solution)/shard_map/ppermute | solution.py:175
  33.7 22.5 %copy-start.12 = (bf16[128,768]{1,0:T(8,128)(2,1)}, bf16[128,768]{1,0:T(8,128)(2,1)S(1)}, u32[]{:S(2)}) copy-start(bf16[128,768]{1,0:T(8,128)(2,1)S(1)} %collective-permute-done.3) | copy-start | bytes 589828
  33.7 10.8 %collective-permute-start.5 = (bf16[128,768]{1,0:T(8,128)(2,1)S(1)}, bf16[128,768]{1,0:T(8,128)(2,1)S(1)}, u32[]{:S(2)}, u32[]{:S(2)}) collective-permute-start(bf16[128,768]{1,0:T(8,128)(2,1)S(1)} %collective-permute-done.3), channel_id=1, source_target_pairs={{0,2},{2,4},{4,6},{6,8},{8,10},{10,12},{12,14},{14,16},{16,18},{18... | collective-permute-start | bytes 589832 | tf_op jit(solution)/shard_map/ppermute | solution.py:175
  34.6 10.8 %collective-permute-start.4 = (bf16[128,768]{1,0:T(8,128)(2,1)S(1)}, bf16[128,768]{1,0:T(8,128)(2,1)S(1)}, u32[]{:S(2)}, u32[]{:S(2)}) collective-permute-start(bf16[128,768]{1,0:T(8,128)(2,1)S(1)} %collective-permute-done.2), channel_id=1, source_target_pairs={{0,254},{2,0},{4,2},{6,4},{8,6},{10,8},{12,10},{14,12},{16,14},{18... | collective-permute-start | bytes 589832 | tf_op jit(solution)/shard_map/ppermute | solution.py:175
  44.5 11.7 %copy-start.14 = (bf16[128,768]{1,0:T(8,128)(2,1)}, bf16[128,768]{1,0:T(8,128)(2,1)S(1)}, u32[]{:S(2)}) copy-start(bf16[128,768]{1,0:T(8,128)(2,1)S(1)} %collective-permute-done.5) | copy-start | bytes 589828
  44.5 10.8 %collective-permute-start.7 = (bf16[128,768]{1,0:T(8,128)(2,1)S(1)}, bf16[128,768]{1,0:T(8,128)(2,1)S(1)}, u32[]{:S(2)}, u32[]{:S(2)}) collective-permute-start(bf16[128,768]{1,0:T(8,128)(2,1)S(1)} %collective-permute-done.5), channel_id=1, source_target_pairs={{0,2},{2,4},{4,6},{6,8},{8,10},{10,12},{12,14},{14,16},{16,18},{18... | collective-permute-start | bytes 589832 | tf_op jit(solution)/shard_map/ppermute | solution.py:175
  45.4 10.8 %collective-permute-start.6 = (bf16[128,768]{1,0:T(8,128)(2,1)S(1)}, bf16[128,768]{1,0:T(8,128)(2,1)S(1)}, u32[]{:S(2)}, u32[]{:S(2)}) collective-permute-start(bf16[128,768]{1,0:T(8,128)(2,1)S(1)} %collective-permute-done.4), channel_id=1, source_target_pairs={{0,254},{2,0},{4,2},{6,4},{8,6},{10,8},{12,10},{14,12},{16,14},{18... | collective-permute-start | bytes 589832 | tf_op jit(solution)/shard_map/ppermute | solution.py:175
  107.1 21.4 %copy-start.25 = (f32[128,128]{1,0:T(8,128)S(1)}, f32[128,128]{1,0:T(8,128)}, u32[]{:S(2)}) copy-start(f32[128,128]{1,0:T(8,128)} %get-tuple-element.15) | copy-start | bytes 196612
  107.2 29.1 %copy-start.19 = (f32[128,128]{1,0:T(8,128)S(1)}, f32[128,128]{1,0:T(8,128)}, u32[]{:S(2)}) copy-start(f32[128,128]{1,0:T(8,128)} %get-tuple-element.12) | copy-start | bytes 196612
  107.2 29.1 %copy-start.26 = (f32[128,128]{1,0:T(8,128)S(1)}, f32[128,128]{1,0:T(8,128)}, u32[]{:S(2)}) copy-start(f32[128,128]{1,0:T(8,128)} %get-tuple-element.13) | copy-start | bytes 196612
  107.2 29.3 %copy-start.20 = (f32[128,128]{1,0:T(8,128)S(1)}, f32[128,128]{1,0:T(8,128)}, u32[]{:S(2)}) copy-start(f32[128,128]{1,0:T(8,128)} %get-tuple-element.14) | copy-start | bytes 196612
  107.2 29.5 %copy-start.23 = (f32[128,128]{1,0:T(8,128)S(1)}, f32[128,128]{1,0:T(8,128)}, u32[]{:S(2)}) copy-start(f32[128,128]{1,0:T(8,128)} %get-tuple-element.16) | copy-start | bytes 196612
  107.2 29.8 %copy-start.24 = (f32[128,128]{1,0:T(8,128)S(1)}, f32[128,128]{1,0:T(8,128)}, u32[]{:S(2)}) copy-start(f32[128,128]{1,0:T(8,128)} %get-tuple-element.17) | copy-start | bytes 196612
  108.3 29.1 %copy-start.21 = (f32[128,128]{1,0:T(8,128)S(1)}, f32[128,128]{1,0:T(8,128)}, u32[]{:S(2)}) copy-start(f32[128,128]{1,0:T(8,128)} %get-tuple-element.19) | copy-start | bytes 196612
  108.3 31.5 %collective-permute-start.15 = (f32[128,768]{1,0:T(8,128)S(1)}, f32[128,768]{1,0:T(8,128)S(1)}, u32[]{:S(2)}, u32[]{:S(2)}) collective-permute-start(f32[128,768]{1,0:T(8,128)S(1)} %convolution_multiply_fusion), channel_id=1, source_target_pairs={{0,248},{2,250},{4,252},{6,254},{8,0},{10,2},{12,4},{14,6},{16,8},... | collective-permute-start | bytes 1179656 | tf_op jit(solution)/shard_map/ppermute | solution.py:175
  117.6 20.0 %copy-start.18 = (f32[128,128]{1,0:T(8,128)S(1)}, f32[128,128]{1,0:T(8,128)}, u32[]{:S(2)}) copy-start(f32[128,128]{1,0:T(8,128)} %get-tuple-element.18) | copy-start | bytes 196612
  117.6 20.0 %copy-start.27 = (s32[1,128]{1,0:T(1,128)S(1)}, s32[1,128]{1,0:T(1,128)}, u32[]{:S(2)}) copy-start(s32[1,128]{1,0:T(1,128)} %param.12) | copy-start | bytes 1540
  117.7 25.4 %collective-permute-start.14 = (f32[128,768]{1,0:T(8,128)S(1)}, f32[128,768]{1,0:T(8,128)S(1)}, u32[]{:S(2)}, u32[]{:S(2)}) collective-permute-start(f32[128,768]{1,0:T(8,128)S(1)} %convolution_multiply_fusion.1), channel_id=1, source_target_pairs={{0,8},{2,10},{4,12},{6,14},{8,16},{10,18},{12,20},{14,22},{16,24},... | collective-permute-start | bytes 1179656 | tf_op jit(solution)/shard_map/ppermute | solution.py:175
  118.9 19.1 %copy-start.17 = (bf16[128,768]{1,0:T(8,128)(2,1)S(1)}, bf16[128,768]{1,0:T(8,128)(2,1)}, u32[]{:S(2)}) copy-start(bf16[128,768]{1,0:T(8,128)(2,1)} %copy-done.16) | copy-start | bytes 589828
  118.9 19.1 %copy-start.22 = (f32[128,128]{1,0:T(8,128)S(1)}, f32[128,128]{1,0:T(8,128)}, u32[]{:S(2)}) copy-start(f32[128,128]{1,0:T(8,128)} %get-tuple-element.11) | copy-start | bytes 196612
  118.9 28.9 %collective-permute-start.13 = (f32[128,768]{1,0:T(8,128)S(1)}, f32[128,768]{1,0:T(8,128)S(1)}, u32[]{:S(2)}, u32[]{:S(2)}) collective-permute-start(f32[128,768]{1,0:T(8,128)S(1)} %convolution_multiply_fusion.2), channel_id=1, source_target_pairs={{0,250},{2,252},{4,254},{6,0},{8,2},{10,4},{12,6},{14,8},{16,10},{... | collective-permute-start | bytes 1179656 | tf_op jit(solution)/shard_map/ppermute | solution.py:175
  128.4 28.0 %collective-permute-start.12 = (f32[128,768]{1,0:T(8,128)S(1)}, f32[128,768]{1,0:T(8,128)S(1)}, u32[]{:S(2)}, u32[]{:S(2)}) collective-permute-start(f32[128,768]{1,0:T(8,128)S(1)} %convolution_multiply_fusion.3), channel_id=1, source_target_pairs={{0,6},{2,8},{4,10},{6,12},{8,14},{10,16},{12,18},{14,20},{16,22},{... | collective-permute-start | bytes 1179656 | tf_op jit(solution)/shard_map/ppermute | solution.py:175
  128.8 27.6 %collective-permute-start.11 = (f32[128,768]{1,0:T(8,128)S(1)}, f32[128,768]{1,0:T(8,128)S(1)}, u32[]{:S(2)}, u32[]{:S(2)}) collective-permute-start(f32[128,768]{1,0:T(8,128)S(1)} %convolution_multiply_fusion.4), channel_id=1, source_target_pairs={{0,252},{2,254},{4,0},{6,2},{8,4},{10,6},{12,8},{14,10},{16,12},{1... | collective-permute-start | bytes 1179656 | tf_op jit(solution)/shard_map/ppermute | solution.py:175
  139.8 23.4 %collective-permute-start.10 = (f32[128,768]{1,0:T(8,128)S(1)}, f32[128,768]{1,0:T(8,128)S(1)}, u32[]{:S(2)}, u32[]{:S(2)}) collective-permute-start(f32[128,768]{1,0:T(8,128)S(1)} %convolution_multiply_fusion.5), channel_id=1, source_target_pairs={{0,4},{2,6},{4,8},{6,10},{8,12},{10,14},{12,16},{14,18},{16,20},{1... | collective-permute-start | bytes 1179656 | tf_op jit(solution)/shard_map/ppermute | solution.py:175
  143.1 20.2 %collective-permute-start.9 = (f32[128,768]{1,0:T(8,128)S(1)}, f32[128,768]{1,0:T(8,128)S(1)}, u32[]{:S(2)}, u32[]{:S(2)}) collective-permute-start(f32[128,768]{1,0:T(8,128)S(1)} %convolution_multiply_fusion.6), channel_id=1, source_target_pairs={{0,254},{2,0},{4,2},{6,4},{8,6},{10,8},{12,10},{14,12},{16,14},{18... | collective-permute-start | bytes 1179656 | tf_op jit(solution)/shard_map/ppermute | solution.py:175
  147.8 15.4 %collective-permute-start.8 = (f32[128,768]{1,0:T(8,128)S(1)}, f32[128,768]{1,0:T(8,128)S(1)}, u32[]{:S(2)}, u32[]{:S(2)}) collective-permute-start(f32[128,768]{1,0:T(8,128)S(1)} %convolution_multiply_fusion.7), channel_id=1, source_target_pairs={{0,2},{2,4},{4,6},{6,8},{8,10},{10,12},{12,14},{14,16},{16,18},{18... | collective-permute-start | bytes 1179656 | tf_op jit(solution)/shard_map/ppermute | solution.py:175
  (13 other events, 68.9 us)
Sparse Core Ops, SparseCore 0:
  57.2 49.8 all-reduce.4

commit v2 on v0

v2 whole, which is shorter than its diff:
```python
import jax
import jax.numpy as jnp
import numpy as np
from jax import lax
from jax.experimental import pallas as pl
from jax.experimental.pallas import tpu as pltpu
from jax.sharding import PartitionSpec as P

MESH = pl.DeviceIdType.MESH
REACH = 4
XS, YS, ZS = 4, 2, 8
GROUP = 2 * YS
MET = 2 * REACH + 1
EXTRA = 16
COPIES = 2 + 8 + 8 + MET + 2 * REACH + 3 + 6 + 2 * (XS - 1) + 2 * (ZS - 1)
LAST = (((1,), (1,)), ((), ()))
FIRST = (((0,), (0,)), ((), ()))
F32, BF16 = jnp.float32, jnp.bfloat16


def column_order():
    order = np.arange(XS * YS * ZS * 2 * 12).reshape(XS, YS, ZS, 2, 12)
    return order.transpose(1, 3, 0, 2, 4).reshape(1, -1).astype(np.int32)


def as_row(column):
    n = column.shape[0]
    return jnp.transpose(jnp.broadcast_to(column, (n, n)))[:8]


def as_column(row):
    n = row.shape[1]
    return jnp.transpose(jnp.broadcast_to(row, (n, n)))[:, :1]


def kernel(
    picture_ref, caption_ref, picture_head_hbm, caption_head_hbm, match_ref, scale_ref, offset_ref, order_ref,
    loss_out, image_out, text_out,
    picture_head, caption_head, raws, norm_out, norm_in, texts, images, part_out, part_in, slope_out, slope_in,
    loss_sum, dot_sum, towers_out, towers, backs, total, x_out, x_in, z_own, z_out, z_in, load, send, recv,
):
    dp, side = lax.axis_index("dp"), lax.axis_index("head")
    core = lax.rem(dp, 2)
    z = lax.rem(lax.div(dp, 2), ZS)
    y = lax.rem(lax.div(dp, 2 * ZS), YS)
    x = lax.div(dp, 2 * ZS * YS)
    blocks = XS * YS * ZS * 2
    rows, columns = picture_ref.shape
    half = picture_head.shape[1]

    head_loads = [
        pltpu.make_async_copy(caption_head_hbm, caption_head, load.at[0]),
        pltpu.make_async_copy(picture_head_hbm, picture_head, load.at[1]),
    ]
    for copy_in in head_loads:
        copy_in.start()

    def place(x, y, z, core):
        return ((x * YS + y) * ZS + z) * 2 + core

    def block(by):
        return (lax.rem(dp + by + blocks, blocks), side)

    peer = (dp, 1 - side)
    sibling = (dp + 1 - 2 * core, side)
    over = (place(x, 1 - y, z, core), side)
    crossed = [(place(x, 1 - y, z, c), 1 - side) for c in range(2)]
    x_peers = [(place(lax.rem(x + d, XS), y, z, core), side) for d in range(1, XS)]
    z_peers = [(place(x, y, lax.rem(z + d, ZS), core), side) for d in range(1, ZS)]
    near = [block(by) for by in range(-REACH, REACH + 1) if by]
    greeted = [peer, over, *crossed, *near, *x_peers, *z_peers]
    barrier = pltpu.get_barrier_semaphore()
    for other in greeted:
        pl.semaphore_signal(barrier, inc=1, device_id=other, device_id_type=MESH)

    used = [0]
    sent = []

    def copy(src, dst, target, arrival=None):
        at = used[0]
        used[0] += 1
        at_arrival = at if arrival is None else arrival
        made = pltpu.make_async_remote_copy(
            src_ref=src, dst_ref=dst, send_sem=send.at[at], recv_sem=recv.at[at_arrival],
            device_id=target, device_id_type=MESH,
        )
        made.start()
        sent.append(made)
        return at

    def landed(dst, at):
        pltpu.make_async_copy(dst, dst, recv.at[at]).wait()

    norm_at = []
    for t, tower_ref, head in ((0, caption_ref, caption_head), (1, picture_ref, picture_head)):
        head_loads[t].wait()
        raw = jnp.dot(tower_ref[...], head[...], preferred_element_type=F32)
        raws[t] = raw
        norm_out[t] = as_row(jnp.sum(raw * raw, axis=1, keepdims=True))
        if t == 0:
            pl.semaphore_wait(barrier, len(greeted))
        norm_at.append(copy(norm_out.at[t], norm_in.at[t], peer))

    def embedding(t):
        landed(norm_in.at[t], norm_at[t])
        inverse = lax.rsqrt(as_column((norm_out[t] + norm_in[t])[:1]) + 1e-06)
        return (raws[t] * inverse).astype(BF16), inverse

    def spread_own(held):
        at = {by: copy(held.at[REACH], held.at[REACH - by], block(by)) for by in (2, -2, 4, -4)}
        at["own"] = copy(held.at[REACH], held.at[REACH + 2 * core - 1], sibling)
        return at

    def arrived(held, at, by):
        landed(held.at[REACH + by], at[-by])

    def hand_over(held, at, name, by):
        at[name] = copy(held.at[REACH + by], held.at[REACH + by - 1 + 2 * core], sibling)

    outer = 4 - 8 * core
    slot_of = {
        "own": REACH + 1 - 2 * core,
        "up": REACH + 3 - 2 * core,
        "down": REACH - 1 - 2 * core,
        "outer": REACH - 3 + 6 * core,
    }

    text_emb, text_inv = embedding(0)
    texts[REACH] = text_emb
    text_at = spread_own(texts)
    image_emb, image_inv = embedding(1)
    images[REACH] = image_emb

    part_at = {}

    def logits(key, slot):
        part_out[slot] = lax.dot_general(images[REACH], texts[slot], LAST, preferred_element_type=F32)
        part_at[key] = copy(part_out.at[slot], part_in.at[slot], peer)

    logits(0, REACH)

    mine = y * 2 + core
    part = columns // GROUP
    wide = columns // XS
    pair = jnp.concatenate([picture_ref[...], caption_ref[...]], axis=0)
    for g in range(GROUP):
        pick = order_ref[:, g * part : (g + 1) * part]
        acc = None
        for b in range(XS):
            chosen = lax.broadcasted_iota(jnp.int32, (wide, part), 0) + b * wide == pick
            one = jnp.where(chosen, 1.0, 0.0).astype(BF16)
            term = jnp.dot(pair[:, b * wide : (b + 1) * wide], one, preferred_element_type=F32)
            acc = term if acc is None else acc + term
        towers_out[g, 0] = acc[:rows].astype(BF16)
        towers_out[g, 1] = acc[rows:].astype(BF16)
    towers[mine] = towers_out[mine]
    cross_slot = (1 - y) * 2
    tower_at = copy(towers_out.at[y * 2 + 1 - core], towers.at[mine], sibling)
    cross_at = used[0]
    for c in range(2):
        copy(towers_out.at[cross_slot + c], towers.at[mine], crossed[c], cross_at + core)

    landed(texts.at[slot_of["own"]], text_at["own"])
    logits("own", slot_of["own"])
    image_at = spread_own(images)

    scale, offset = scale_ref[0], offset_ref[0]
    match = as_column(match_ref[...].astype(F32))
    positive = jnp.where(
        lax.broadcasted_iota(jnp.int32, (rows, rows), 1).astype(F32) == match, 1.0, 0.0
    )
    slope_at = {}

    def slopes(key, slot, by):
        landed(part_in.at[slot], part_at[key])
        product = scale * (part_out[slot] + part_in[slot])
        logit = product + offset
        small = jnp.exp(-jnp.abs(logit))
        inverse = 1.0 / (1.0 + small)
        sigmoid = jnp.where(logit >= 0.0, inverse, small * inverse)
        loss = jnp.maximum(logit, 0.0) + jnp.log1p(small)
        if key == 0:
            sigmoid = sigmoid - positive
            loss = loss - positive * logit
        slope = (sigmoid * (1.0 / rows)).astype(BF16)
        weighted = slope.astype(F32) * product
        if key == 0:
            loss_sum[...] = loss
            dot_sum[...] = weighted
        else:
            loss_sum[...] += loss
            dot_sum[...] += weighted
        over_images = jnp.sum(weighted, axis=0, keepdims=True)
        high = over_images.astype(BF16).astype(F32)
        middle = (over_images - high).astype(BF16).astype(F32)
        low = over_images - high - middle
        extra = jnp.concatenate([high, middle, low, jnp.zeros((EXTRA - 3, rows), F32)], axis=0)
        slope_out[slot, :rows] = slope
        slope_out[slot, rows:] = extra.astype(BF16)
        if key == 0:
            slope_in[REACH] = slope_out[REACH]
        else:
            slope_at[key] = copy(slope_out.at[slot], slope_in.at[2 * REACH - slot], block(by))

    slopes(0, REACH, 0)
    for name, by in (("up", 2), ("down", -2)):
        arrived(texts, text_at, by)
        hand_over(texts, text_at, name, by)
        logits(by, REACH + by)
    slopes("own", slot_of["own"], 1 - 2 * core)
    for by in (4, -4):
        arrived(texts, text_at, by)
        logits(by, REACH + by)
    hand_over(texts, text_at, "outer", outer)
    for name in ("up", "down"):
        landed(texts.at[slot_of[name]], text_at[name])
        logits(name, slot_of[name])
    for by in (2, -2):
        slopes(by, REACH + by, by)
    for name, by in (("up", 2), ("down", -2)):
        arrived(images, image_at, by)
        hand_over(images, image_at, name, by)
    for by in (4, -4):
        slopes(by, REACH + by, by)
    landed(texts.at[slot_of["outer"]], text_at["outer"])
    logits("outer", slot_of["outer"])
    for name in ("up", "down"):
        slopes(name, slot_of[name], slot_of[name] - REACH)
    for by in (4, -4):
        arrived(images, image_at, by)
    hand_over(images, image_at, "outer", outer)
    slopes("outer", slot_of["outer"], slot_of["outer"] - REACH)

    def back_through(gradient, emb, dot, inverse):
        return ((scale * gradient - emb.astype(F32) * dot) * inverse).astype(BF16)

    across = jnp.concatenate([slope_out[k, :rows] for k in range(MET)], axis=1)
    gradient = jnp.dot(across, texts[...].reshape(MET * rows, half), preferred_element_type=F32)
    image_dot = jnp.sum(dot_sum[...], axis=1, keepdims=True)
    backs[0, mine] = back_through(gradient, images[REACH], image_dot, image_inv)
    back_at = {}

    def spread_back(t):
        back_at[t, "over"] = copy(backs.at[t, mine], backs.at[t, mine], over)
        back_at[t, "sibling"] = copy(backs.at[t, mine], backs.at[t, mine], sibling)

    spread_back(0)
    loss_out[...] = as_row(jnp.sum(loss_sum[...], axis=1, keepdims=True))[:1] * (1.0 / rows)

    came = {-2: -2, 2: 2, -4: -4, 4: 4, "own": None, "up": None, "down": None, "outer": None}
    slope_slot = {
        "own": REACH + 1 - 2 * core,
        "up": REACH - 1 - 2 * core,
        "down": REACH + 3 - 2 * core,
        "outer": REACH - 3 + 6 * core,
    }
    for name in came:
        slot = REACH - name if came[name] else slope_slot[name]
        landed(slope_in.at[slot], slope_at[name])
    for name in slot_of:
        landed(images.at[slot_of[name]], image_at[name])
    text_dot = None
    for k in range(MET):
        rows3 = jnp.sum(slope_in[k, rows:].astype(F32), axis=0, keepdims=True)
        text_dot = rows3 if text_dot is None else text_dot + rows3
    down = jnp.concatenate([slope_in[k, :rows] for k in range(MET)], axis=0)
    gradient = lax.dot_general(
        down, images[...].reshape(MET * rows, half), FIRST, preferred_element_type=F32
    )
    backs[1, mine] = back_through(gradient, texts[REACH], as_column(text_dot), text_inv)
    spread_back(1)

    far = cross_slot + core
    for t in range(2):
        landed(backs.at[t, far], back_at[t, "over"])
        back_at[t, "passed"] = copy(backs.at[t, far], backs.at[t, far], sibling)
    landed(towers.at[y * 2 + 1 - core], tower_at)
    for c in range(2):
        landed(towers.at[cross_slot + c], cross_at + c)
    x_at = {}
    for t in range(2):
        landed(backs.at[t, y * 2 + 1 - core], back_at[t, "sibling"])
        landed(backs.at[t, cross_slot + 1 - core], back_at[t, "passed"])
        product = lax.dot_general(
            towers[:, t].reshape(GROUP * rows, part), backs[t].reshape(GROUP * rows, half),
            FIRST, preferred_element_type=F32,
        ).reshape(XS, part // XS, half)
        total[t] = product
        x_out[t] = product.astype(BF16)
        for d in range(1, XS):
            x_at[t, d] = copy(x_out.at[t, lax.rem(x + d, XS)], x_in.at[t, d - 1], x_peers[d - 1])
    z_at = {}
    for t in range(2):
        value = total[t, x]
        for d in range(1, XS):
            landed(x_in.at[t, d - 1], x_at[t, d])
            value = value + x_in[t, d - 1].astype(F32)
        for c in range(ZS):
            chunk = value[c * 12 : (c + 1) * 12]
            chunk = jnp.concatenate([chunk, jnp.zeros((4, half), F32)], axis=0)
            z_own[t, c] = chunk
            z_out[t, c] = chunk.astype(BF16)
        for d in range(1, ZS):
            z_at[t, d] = copy(z_out.at[t, lax.rem(z + d, ZS)], z_in.at[t, d - 1], z_peers[d - 1])
    for t, out in ((0, image_out), (1, text_out)):
        value = z_own[t, z]
        for d in range(1, ZS):
            landed(z_in.at[t, d - 1], z_at[t, d])
            value = value + z_in[t, d - 1].astype(F32)
        out[...] = value[:12]
    for made in sent:
        made.wait_send()


def shards(
    picture_tower_summary,
    caption_tower_summary,
    picture_head_matrix,
    caption_head_matrix,
    matching_caption_row,
    affinity_scale,
    affinity_offset,
):
    rows, columns = picture_tower_summary.shape
    half = picture_head_matrix.shape[1]
    part = columns // GROUP
    vmem = pl.BlockSpec(memory_space=pltpu.VMEM)
    smem = pl.BlockSpec(memory_space=pltpu.SMEM)
    hbm = pl.BlockSpec(memory_space=pl.ANY)
    loss, image_grad_w, text_grad_w = pl.pallas_call(
        kernel,
        out_shape=[
            jax.ShapeDtypeStruct((1, rows), F32),
            jax.ShapeDtypeStruct((12, half), F32),
            jax.ShapeDtypeStruct((12, half), F32),
        ],
        in_specs=[vmem, vmem, hbm, hbm, vmem, smem, smem, vmem],
        out_specs=[vmem] * 3,
        scratch_shapes=[
            pltpu.VMEM((columns, half), BF16),
            pltpu.VMEM((columns, half), BF16),
            pltpu.VMEM((2, rows, half), F32),
            pltpu.VMEM((2, 8, rows), F32),
            pltpu.VMEM((2, 8, rows), F32),
            pltpu.VMEM((MET, rows, half), BF16),
            pltpu.VMEM((MET, rows, half), BF16),
            pltpu.VMEM((MET, rows, rows), F32),
            pltpu.VMEM((MET, rows, rows), F32),
            pltpu.VMEM((MET, rows + EXTRA, rows), BF16),
            pltpu.VMEM((MET, rows + EXTRA, rows), BF16),
            pltpu.VMEM((rows, rows), F32),
            pltpu.VMEM((rows, rows), F32),
            pltpu.VMEM((GROUP, 2, rows, part), BF16),
            pltpu.VMEM((GROUP, 2, rows, part), BF16),
            pltpu.VMEM((2, GROUP, rows, half), BF16),
            pltpu.VMEM((2, XS, part // XS, half), F32),
            pltpu.VMEM((2, XS, part // XS, half), BF16),
            pltpu.VMEM((2, XS - 1, part // XS, half), BF16),
            pltpu.VMEM((2, ZS, 16, half), F32),
            pltpu.VMEM((2, ZS, 16, half), BF16),
            pltpu.VMEM((2, ZS - 1, 16, half), BF16),
            pltpu.SemaphoreType.DMA((2,)),
            pltpu.SemaphoreType.DMA((COPIES,)),
            pltpu.SemaphoreType.DMA((COPIES,)),
        ],
        compiler_params=pltpu.CompilerParams(
            collective_id=0, has_side_effects=True, vmem_limit_bytes=56 * 1024 * 1024
        ),
    )(
        picture_tower_summary, caption_tower_summary, picture_head_matrix, caption_head_matrix,
        matching_caption_row, affinity_scale, affinity_offset, jnp.asarray(column_order()),
    )
    return loss[0], image_grad_w, text_grad_w


def solution(mesh):
    return jax.shard_map(
        shards,
        mesh=mesh,
        in_specs=(
            P("dp", None),
            P("dp", None),
            P(None, "head"),
            P(None, "head"),
            P("dp", None),
            P(),
            P(),
        ),
        out_specs=(P("dp"), P("dp", "head"), P("dp", "head")),
        check_vma=False,
    )
```

time: 1490 us -> 86.9 us (0.06)
  waiting for transfers between devices: 1350 us -> 0 us
  Pallas kernels: 0 us -> 80.7 us
  starting transfers between devices: 59.8 us -> 0 us
  matrix products: 29.2 us -> 0 us
    unnamed x3 -> x0, waiting for transfers between devices: 1290 us -> none
    pallas_call x0 -> x1, Pallas kernels: none -> 80.7 us  [shards(): pl.pallas_call(kernel, out_shape=[jax.ShapeDtypeStruct((1, rows), F32), j...]
    ppermute x16 -> x0, starting transfers between devices: 59.7 us -> none  [shifted(): lax.ppermute(value, axis, [(i, (i + by) % peers) for i in range(peers)])]
    psum x1 -> x0, waiting for transfers between devices: 48.7 us -> none  [visit(): lax.psum(partial_value, 'head')]
    dot_general x31 -> x0, matrix products: 29.2 us -> none  [the longest x9 10.7 us: visit(): lax.dot_general(logit_slopes, image_emb, contract_first, preferred_elemen...]
    ppermute x16 -> x0, waiting for transfers between devices: 17 us -> none  [shifted(): lax.ppermute(value, axis, [(i, (i + by) % peers) for i in range(peers)])]
  transfers between devices with their start and end apart: 18 -> 0, of which waited for: 6 -> 0; matrix products, arithmetic and copies ran while one was open for 1% -> 0% of each run, Pallas kernels for 0% -> 0%
where the time goes in v2:
time: 86.9 us; the launch traced here: 86.6 us
  Pallas kernels  80.7 us (93%)
  local copies, waits for them, and re-layouts  4.03 us (5%)
  between operations  1.93 us (2%)
    pallas_call x1, Pallas kernels, shards(): pl.pallas_call(kernel, out_shape=[jax.ShapeDtypeStruct((1, rows), F32), j...  80.7 us
    unnamed x3, local copies, waits for them, and re-layouts  4.03 us

profile of v2, /device:TPU:1, one launch (start us, length us, event | category | flops | bytes accessed | tf_op | source)
XLA Modules:
  0.0 86.6 jit_solution(12319821102683625894)
XLA Ops:
  1.9 80.7 %shard_map.103 = (f32[1,128]{1,0:T(1,128)}, f32[12,768]{1,0:T(8,128)}, f32[12,768]{1,0:T(8,128)}) custom-call(bf16[128,1536]{1,0:T(8,128)(2,1)} %picture_ref.1, bf16[128,1536]{1,0:T(8,128)(2,1)} %caption_ref.1, bf16[1536,768]{1,0:T(8,128)(2,1)} %picture_head_hbm.1, bf16[1536,768]{1,0:T(8,128)(2,1)} %caption_head_hbm.1, s32[1,128]{1,0:T(1,128)} %match_ref.1, ...), custom_call_target="tpu_custom_call" | custom-call | tf_op jit(solution)/shard_map/pallas_call | solution.py:330
  82.6 1.2 %copy.16 = f32[128]{0:T(128)} copy(f32[128]{0:T(128)} %bitcast.1) | data formatting | bytes 1024
  83.8 1.4 %copy.17 = f32[12,768]{1,0:T(8,128)} copy(f32[12,768]{1,0:T(8,128)} %get-tuple-element.13) | data formatting | bytes 73728
  85.2 1.4 %copy.18 = f32[12,768]{1,0:T(8,128)} copy(f32[12,768]{1,0:T(8,128)} %get-tuple-element.14) | data formatting | bytes 73728

commit v3 on v2

v3 whole, which is shorter than its diff:
```python
import jax
import jax.numpy as jnp
import numpy as np
from jax import lax
from jax.experimental import pallas as pl
from jax.experimental.pallas import tpu as pltpu
from jax.sharding import PartitionSpec as P

MESH = pl.DeviceIdType.MESH
REACH = 4
XS, YS, ZS = 4, 2, 8
GROUP = 2 * YS
MET = 2 * REACH + 1
EXTRA = 16
CHUNKS = 2
COPIES = 2 + 2 * (7 * CHUNKS + 1) + MET + 2 * REACH + 3 + 12 + 4 * (XS - 1) + 4 * (ZS - 1)
PARTS = 32000.0
LAST = (((1,), (1,)), ((), ()))
FIRST = (((0,), (0,)), ((), ()))
F32, BF16 = jnp.float32, jnp.bfloat16


def column_order():
    order = np.arange(XS * YS * ZS * 2 * 12).reshape(XS, YS, ZS, 2, 12)
    return order.transpose(1, 3, 0, 2, 4).reshape(1, -1).astype(np.int32)


def as_row(column):
    n = column.shape[0]
    return jnp.transpose(jnp.broadcast_to(column, (n, n)))[:8]


def as_column(row):
    n = row.shape[1]
    return jnp.transpose(jnp.broadcast_to(row, (n, n)))[:, :1]


def kernel(
    picture_hbm, caption_hbm, picture_head_hbm, caption_head_hbm, match_ref, scale_ref, offset_ref, order_ref,
    loss_out, image_out, text_out,
    picture_ref, caption_ref, picture_head, caption_head, raws, norm_out, norm_in, texts, images, part_own, part_out, part_in, slope_out, slope_in,
    loss_sum, dot_sum, towers_out, towers, backs, total, x_out, x_in, z_own, z_out, z_in, load, send, recv,
):
    dp, side = lax.axis_index("dp"), lax.axis_index("head")
    core = lax.rem(dp, 2)
    z = lax.rem(lax.div(dp, 2), ZS)
    y = lax.rem(lax.div(dp, 2 * ZS), YS)
    x = lax.div(dp, 2 * ZS * YS)
    blocks = XS * YS * ZS * 2
    rows, columns = picture_ref.shape
    half = picture_head.shape[1]

    loads = [
        pltpu.make_async_copy(caption_hbm, caption_ref, load.at[0]),
        pltpu.make_async_copy(caption_head_hbm, caption_head, load.at[1]),
        pltpu.make_async_copy(picture_hbm, picture_ref, load.at[2]),
        pltpu.make_async_copy(picture_head_hbm, picture_head, load.at[3]),
    ]
    for copy_in in loads:
        copy_in.start()

    def place(x, y, z, core):
        return ((x * YS + y) * ZS + z) * 2 + core

    def block(by):
        return (lax.rem(dp + by + blocks, blocks), side)

    peer = (dp, 1 - side)
    sibling = (dp + 1 - 2 * core, side)
    over = (place(x, 1 - y, z, core), side)
    crossed = [(place(x, 1 - y, z, c), 1 - side) for c in range(2)]
    x_peers = [(place(lax.rem(x + d, XS), y, z, core), side) for d in range(1, XS)]
    z_peers = [(place(x, y, lax.rem(z + d, ZS), core), side) for d in range(1, ZS)]
    near = [block(by) for by in range(-REACH, REACH + 1) if by]
    greeted = [peer, over, *crossed, *near, *x_peers, *z_peers]
    barrier = pltpu.get_barrier_semaphore()
    for other in greeted:
        pl.semaphore_signal(barrier, inc=1, device_id=other, device_id_type=MESH)

    mine = y * 2 + core
    cross_slot = (1 - y) * 2
    part = columns // GROUP
    wide = columns // XS
    cut = half // 2
    used = [0]
    sent = []

    def copy(src, dst, target, arrival=None):
        at = used[0]
        used[0] += 1
        at_arrival = at if arrival is None else arrival
        made = pltpu.make_async_remote_copy(
            src_ref=src, dst_ref=dst, send_sem=send.at[at], recv_sem=recv.at[at_arrival],
            device_id=target, device_id_type=MESH,
        )
        made.start()
        sent.append(made)
        return at

    def landed(dst, at):
        pltpu.make_async_copy(dst, dst, recv.at[at]).wait()

    norm_at = []
    for t, tower_ref, head in ((0, caption_ref, caption_head), (1, picture_ref, picture_head)):
        loads[2 * t].wait()
        loads[2 * t + 1].wait()
        raw = jnp.dot(tower_ref[...], head[...], preferred_element_type=F32)
        raws[t] = raw
        norm_out[t] = as_row(jnp.sum(raw * raw, axis=1, keepdims=True))
        if t == 0:
            pl.semaphore_wait(barrier, len(greeted))
        norm_at.append(copy(norm_out.at[t], norm_in.at[t], peer))

    def embedding(t):
        landed(norm_in.at[t], norm_at[t])
        inverse = lax.rsqrt(as_column((norm_out[t] + norm_in[t])[:1]) + 1e-06)
        return (raws[t] * inverse).astype(BF16), inverse

    size = rows // CHUNKS

    def piece(held, slot, c):
        return held.at[slot, pl.ds(c * size, size)]

    def spread_own(held):
        at = {}
        for c in range(CHUNKS):
            for by in (2, -2):
                at[by, c] = copy(piece(held, REACH, c), piece(held, REACH - by, c), block(by))
        at["own"] = copy(held.at[REACH], held.at[REACH + 2 * core - 1], sibling)
        return at

    def relay(held, at):
        for c in range(CHUNKS):
            for by in (2, -2):
                landed(piece(held, REACH - by, c), at[by, c])
                at["on", by, c] = copy(piece(held, REACH - by, c), piece(held, REACH - 2 * by, c), block(by))
            for name, by in (("up", 2), ("down", -2)):
                hand_over(held, at, name, by, c)

    def relayed(held, at):
        for c in range(CHUNKS):
            for by in (2, -2):
                landed(piece(held, REACH - 2 * by, c), at["on", by, c])
            hand_over(held, at, "outer", outer, c)

    def hand_over(held, at, name, by, c):
        at[name, c] = copy(piece(held, REACH + by, c), piece(held, REACH + by - 1 + 2 * core, c), sibling)

    def handed(held, at, name):
        for c in range(CHUNKS):
            landed(piece(held, slot_of[name], c), at[name, c])

    outer = 4 - 8 * core
    slot_of = {
        "own": REACH + 1 - 2 * core,
        "up": REACH + 3 - 2 * core,
        "down": REACH - 1 - 2 * core,
        "outer": REACH - 3 + 6 * core,
    }

    pair = jnp.concatenate([picture_ref[...], caption_ref[...]], axis=0)
    for g in range(GROUP):
        pick = order_ref[:, g * part : (g + 1) * part]
        acc = None
        for b in range(XS):
            chosen = lax.broadcasted_iota(jnp.int32, (wide, part), 0) + b * wide == pick
            one = jnp.where(chosen, 1.0, 0.0).astype(BF16)
            term = jnp.dot(pair[:, b * wide : (b + 1) * wide], one, preferred_element_type=F32)
            acc = term if acc is None else acc + term
        towers_out[g, 0] = acc[:rows].astype(BF16)
        towers_out[g, 1] = acc[rows:].astype(BF16)
    towers[mine] = towers_out[mine]
    tower_at = copy(towers_out.at[y * 2 + 1 - core], towers.at[mine], sibling)
    cross_at = used[0]
    for c in range(2):
        copy(towers_out.at[cross_slot + c], towers.at[mine], crossed[c], cross_at + core)


    text_emb, text_inv = embedding(0)
    texts[REACH] = text_emb
    text_at = spread_own(texts)
    image_emb, image_inv = embedding(1)
    images[REACH] = image_emb

    part_at = {}

    def logits(key, slot):
        value = lax.dot_general(images[REACH], texts[slot], LAST, preferred_element_type=F32)
        part_own[slot] = value
        part_out[slot] = jnp.round(value * PARTS).astype(jnp.int32).astype(jnp.int16)
        part_at[key] = copy(part_out.at[slot], part_in.at[slot], peer)

    scale, offset = scale_ref[0], offset_ref[0]
    match = as_column(match_ref[...].astype(F32))
    positive = jnp.where(
        lax.broadcasted_iota(jnp.int32, (rows, rows), 1).astype(F32) == match, 1.0, 0.0
    )
    slope_at = {}

    def slopes(key, slot, by):
        landed(part_in.at[slot], part_at[key])
        other = part_in[slot].astype(jnp.int32).astype(F32) * (1.0 / PARTS)
        product = scale * (part_own[slot] + other)
        logit = product + offset
        small = jnp.exp(-jnp.abs(logit))
        inverse = 1.0 / (1.0 + small)
        sigmoid = jnp.where(logit >= 0.0, inverse, small * inverse)
        loss = jnp.maximum(logit, 0.0) + jnp.log1p(small)
        if key == 0:
            sigmoid = sigmoid - positive
            loss = loss - positive * logit
        slope = (sigmoid * (1.0 / rows)).astype(BF16)
        weighted = slope.astype(F32) * product
        if key == 0:
            loss_sum[...] = loss
            dot_sum[...] = weighted
        else:
            loss_sum[...] += loss
            dot_sum[...] += weighted
        over_images = jnp.sum(weighted, axis=0, keepdims=True)
        high = over_images.astype(BF16).astype(F32)
        middle = (over_images - high).astype(BF16).astype(F32)
        low = over_images - high - middle
        extra = jnp.concatenate([high, middle, low, jnp.zeros((EXTRA - 3, rows), F32)], axis=0)
        slope_out[slot, :rows] = slope
        slope_out[slot, rows:] = extra.astype(BF16)
        if key == 0:
            slope_in[REACH] = slope_out[REACH]
        else:
            slope_at[key] = copy(slope_out.at[slot], slope_in.at[2 * REACH - slot], block(by))

    logits(0, REACH)
    landed(texts.at[slot_of["own"]], text_at["own"])
    logits("own", slot_of["own"])
    relay(texts, text_at)
    image_at = spread_own(images)
    for by in (2, -2):
        logits(by, REACH + by)
    slopes(0, REACH, 0)
    slopes("own", slot_of["own"], 1 - 2 * core)
    for name in ("up", "down"):
        handed(texts, text_at, name)
        logits(name, slot_of[name])
    relayed(texts, text_at)
    for by in (4, -4):
        logits(by, REACH + by)
    handed(texts, text_at, "outer")
    logits("outer", slot_of["outer"])
    relay(images, image_at)
    for by in (2, -2):
        slopes(by, REACH + by, by)
    for name in ("up", "down"):
        slopes(name, slot_of[name], slot_of[name] - REACH)
    for by in (4, -4):
        slopes(by, REACH + by, by)
    slopes("outer", slot_of["outer"], slot_of["outer"] - REACH)

    def back_through(gradient, emb, dot, inverse):
        return ((scale * gradient - emb.astype(F32) * dot) * inverse).astype(BF16)

    across = jnp.concatenate([slope_out[k, :rows] for k in range(MET)], axis=1)
    gradient = jnp.dot(across, texts[...].reshape(MET * rows, half), preferred_element_type=F32)
    image_dot = jnp.sum(dot_sum[...], axis=1, keepdims=True)
    back = back_through(gradient, images[REACH], image_dot, image_inv)
    back_at = {}

    def spread_back(t, back):
        for h in range(2):
            backs[t, h, mine] = back[:, h * cut : (h + 1) * cut]
            back_at[t, h, "over"] = copy(backs.at[t, h, mine], backs.at[t, h, mine], over)
        for h in range(2):
            back_at[t, h, "sibling"] = copy(backs.at[t, h, mine], backs.at[t, h, mine], sibling)

    spread_back(0, back)
    loss_out[...] = as_row(jnp.sum(loss_sum[...], axis=1, keepdims=True))[:1] * (1.0 / rows)

    relayed(images, image_at)

    came = {-2: -2, 2: 2, -4: -4, 4: 4, "own": None, "up": None, "down": None, "outer": None}
    slope_slot = {
        "own": REACH + 1 - 2 * core,
        "up": REACH - 1 - 2 * core,
        "down": REACH + 3 - 2 * core,
        "outer": REACH - 3 + 6 * core,
    }
    for name in came:
        slot = REACH - name if came[name] else slope_slot[name]
        landed(slope_in.at[slot], slope_at[name])
    landed(images.at[slot_of["own"]], image_at["own"])
    for name in ("up", "down", "outer"):
        handed(images, image_at, name)
    text_dot = None
    for k in range(MET):
        rows3 = jnp.sum(slope_in[k, rows:].astype(F32), axis=0, keepdims=True)
        text_dot = rows3 if text_dot is None else text_dot + rows3
    down = jnp.concatenate([slope_in[k, :rows] for k in range(MET)], axis=0)
    gradient = lax.dot_general(
        down, images[...].reshape(MET * rows, half), FIRST, preferred_element_type=F32
    )
    spread_back(1, back_through(gradient, texts[REACH], as_column(text_dot), text_inv))

    far = cross_slot + core
    landed(towers.at[y * 2 + 1 - core], tower_at)
    for c in range(2):
        landed(towers.at[cross_slot + c], cross_at + c)
    x_at = {}
    parts = [(t, h) for t in range(2) for h in range(2)]
    for t, h in parts:
        held = backs.at[t, h]
        landed(held.at[far], back_at[t, h, "over"])
        passed = copy(held.at[far], held.at[far], sibling)
        landed(held.at[y * 2 + 1 - core], back_at[t, h, "sibling"])
        landed(held.at[cross_slot + 1 - core], passed)
        product = lax.dot_general(
            towers[:, t].reshape(GROUP * rows, part), backs[t, h].reshape(GROUP * rows, cut),
            FIRST, preferred_element_type=F32,
        ).reshape(XS, part // XS, cut)
        total[t, h] = product
        x_out[t, h] = product.astype(BF16)
        for d in range(1, XS):
            x_at[t, h, d] = copy(x_out.at[t, h, lax.rem(x + d, XS)], x_in.at[t, h, d - 1], x_peers[d - 1])
    z_at = {}
    for t, h in parts:
        value = total[t, h, x]
        for d in range(1, XS):
            landed(x_in.at[t, h, d - 1], x_at[t, h, d])
            value = value + x_in[t, h, d - 1].astype(F32)
        for c in range(ZS):
            chunk = value[c * 12 : (c + 1) * 12]
            chunk = jnp.concatenate([chunk, jnp.zeros((4, cut), F32)], axis=0)
            z_own[t, h, c] = chunk
            z_out[t, h, c] = chunk.astype(BF16)
        for d in range(1, ZS):
            z_at[t, h, d] = copy(z_out.at[t, h, lax.rem(z + d, ZS)], z_in.at[t, h, d - 1], z_peers[d - 1])
    for t, h in parts:
        value = z_own[t, h, z]
        for d in range(1, ZS):
            landed(z_in.at[t, h, d - 1], z_at[t, h, d])
            value = value + z_in[t, h, d - 1].astype(F32)
        (image_out, text_out)[t][:, h * cut : (h + 1) * cut] = value[:12]
    for made in sent:
        made.wait_send()


def results(loss_ref, image_ref, text_ref, loss_out, image_out, text_out):
    loss_out[...] = loss_ref[...]
    image_out[...] = image_ref[...]
    text_out[...] = text_ref[...]


def shards(
    picture_tower_summary,
    caption_tower_summary,
    picture_head_matrix,
    caption_head_matrix,
    matching_caption_row,
    affinity_scale,
    affinity_offset,
):
    rows, columns = picture_tower_summary.shape
    half = picture_head_matrix.shape[1]
    part = columns // GROUP
    vmem = pl.BlockSpec(memory_space=pltpu.VMEM)
    smem = pl.BlockSpec(memory_space=pltpu.SMEM)
    hbm = pl.BlockSpec(memory_space=pl.ANY)
    loss, image_grad_w, text_grad_w = pl.pallas_call(
        kernel,
        out_shape=[
            jax.ShapeDtypeStruct((1, rows), F32),
            jax.ShapeDtypeStruct((12, half), F32),
            jax.ShapeDtypeStruct((12, half), F32),
        ],
        in_specs=[hbm, hbm, hbm, hbm, vmem, smem, smem, vmem],
        out_specs=[vmem] * 3,
        scratch_shapes=[
            pltpu.VMEM((rows, columns), BF16),
            pltpu.VMEM((rows, columns), BF16),
            pltpu.VMEM((columns, half), BF16),
            pltpu.VMEM((columns, half), BF16),
            pltpu.VMEM((2, rows, half), F32),
            pltpu.VMEM((2, 8, rows), F32),
            pltpu.VMEM((2, 8, rows), F32),
            pltpu.VMEM((MET, rows, half), BF16),
            pltpu.VMEM((MET, rows, half), BF16),
            pltpu.VMEM((MET, rows, rows), F32),
            pltpu.VMEM((MET, rows, rows), jnp.int16),
            pltpu.VMEM((MET, rows, rows), jnp.int16),
            pltpu.VMEM((MET, rows + EXTRA, rows), BF16),
            pltpu.VMEM((MET, rows + EXTRA, rows), BF16),
            pltpu.VMEM((rows, rows), F32),
            pltpu.VMEM((rows, rows), F32),
            pltpu.VMEM((GROUP, 2, rows, part), BF16),
            pltpu.VMEM((GROUP, 2, rows, part), BF16),
            pltpu.VMEM((2, 2, GROUP, rows, half // 2), BF16),
            pltpu.VMEM((2, 2, XS, part // XS, half // 2), F32),
            pltpu.VMEM((2, 2, XS, part // XS, half // 2), BF16),
            pltpu.VMEM((2, 2, XS - 1, part // XS, half // 2), BF16),
            pltpu.VMEM((2, 2, ZS, 16, half // 2), F32),
            pltpu.VMEM((2, 2, ZS, 16, half // 2), BF16),
            pltpu.VMEM((2, 2, ZS - 1, 16, half // 2), BF16),
            pltpu.SemaphoreType.DMA((4,)),
            pltpu.SemaphoreType.DMA((COPIES,)),
            pltpu.SemaphoreType.DMA((COPIES,)),
        ],
        compiler_params=pltpu.CompilerParams(
            collective_id=0, has_side_effects=True, vmem_limit_bytes=56 * 1024 * 1024
        ),
    )(
        picture_tower_summary, caption_tower_summary, picture_head_matrix, caption_head_matrix,
        matching_caption_row, affinity_scale, affinity_offset, jnp.asarray(column_order()),
    )
    loss, image_grad_w, text_grad_w = pl.pallas_call(
        results,
        out_shape=[
            jax.ShapeDtypeStruct((1, rows), F32),
            jax.ShapeDtypeStruct((12, half), F32),
            jax.ShapeDtypeStruct((12, half), F32),
        ],
        in_specs=[vmem] * 3,
        out_specs=[vmem] * 3,
    )(loss, image_grad_w, text_grad_w)
    return loss[0], image_grad_w, text_grad_w


def solution(mesh):
    return jax.shard_map(
        shards,
        mesh=mesh,
        in_specs=(
            P("dp", None),
            P("dp", None),
            P(None, "head"),
            P(None, "head"),
            P("dp", None),
            P(),
            P(),
        ),
        out_specs=(P("dp"), P("dp", "head"), P("dp", "head")),
        check_vma=False,
    )
```

time: 86.9 us -> 76 us (0.87)
  Pallas kernels: 80.7 us -> 73.9 us
  local copies, waits for them, and re-layouts: 4.03 us -> 0 us
    pallas_call x1, Pallas kernels: 80.7 us -> 72.4 us  [shards(): pl.pallas_call(kernel, out_shape=[jax.ShapeDtypeStruct((1, rows), F32), j...]
    unnamed x3 -> x0, local copies, waits for them, and re-layouts: 4.03 us -> none
    pallas_call x0 -> x1, Pallas kernels: none -> 1.47 us  [shards(): pl.pallas_call(results, out_shape=[jax.ShapeDtypeStruct((1, rows), F32),...]
where the time goes in v3:
time: 76 us; the launch traced here: 75.9 us
  Pallas kernels  73.9 us (97%)
  between operations  1.93 us (3%)
    pallas_call x1, Pallas kernels, shards(): pl.pallas_call(kernel, out_shape=[jax.ShapeDtypeStruct((1, rows), F32), j...  72.4 us

profile of v3, /device:TPU:1, one launch (start us, length us, event | category | flops | bytes accessed | tf_op | source)
XLA Modules:
  0.0 75.9 jit_solution(18066657424550524418)
XLA Ops:
  1.9 72.4 %shard_map.103 = (f32[1,128]{1,0:T(1,128)}, f32[12,768]{1,0:T(8,128)}, f32[12,768]{1,0:T(8,128)}) custom-call(bf16[128,1536]{1,0:T(8,128)(2,1)} %picture_hbm.1, bf16[128,1536]{1,0:T(8,128)(2,1)} %caption_hbm.1, bf16[1536,768]{1,0:T(8,128)(2,1)} %picture_head_hbm.1, bf16[1536,768]{1,0:T(8,128)(2,1)} %caption_head_hbm.1, s32[1,128]{1,0:T(1,128)} %match_ref.1, ...), custom_call_target="tpu_custom_call" | custom-call | tf_op jit(solution)/shard_map/pallas_call | solution.py:366
  74.4 1.5 %shard_map.104 = (f32[1,128]{1,0:T(1,128)}, f32[12,768]{1,0:T(8,128)}, f32[12,768]{1,0:T(8,128)}) custom-call(f32[1,128]{1,0:T(1,128)} %get-tuple-element.9.loss_ref, f32[12,768]{1,0:T(8,128)} %get-tuple-element.10.image_ref, f32[12,768]{1,0:T(8,128)} %get-tuple-element.11.text_ref), custom_call_target="tpu_custom_call" | custom-call | tf_op jit(solution)/shard_map/pallas_call | solution.py:412

commit v4 on v3

--- a/solution.py
+++ b/solution.py
@@ -246,7 +246,6 @@
         logits(by, REACH + by)
     handed(texts, text_at, "outer")
     logits("outer", slot_of["outer"])
-    relay(images, image_at)
     for by in (2, -2):
         slopes(by, REACH + by, by)
     for name in ("up", "down"):
@@ -255,6 +254,7 @@
         slopes(by, REACH + by, by)
     slopes("outer", slot_of["outer"], slot_of["outer"] - REACH)
 
+    relay(images, image_at)
     def back_through(gradient, emb, dot, inverse):
         return ((scale * gradient - emb.astype(F32) * dot) * inverse).astype(BF16)
 

time: 76 us -> 74.3 us (0.978)
  Pallas kernels: 73.9 us -> 72 us
    pallas_call x1, Pallas kernels: 72.4 us -> 70.6 us  [shards(): pl.pallas_call(kernel, out_shape=[jax.ShapeDtypeStruct((1, rows), F32), j...]
where the time goes in v4:
time: 74.3 us; the launch traced here: 74 us
  Pallas kernels  72 us (97%)
  between operations  1.93 us (3%)
    pallas_call x1, Pallas kernels, shards(): pl.pallas_call(kernel, out_shape=[jax.ShapeDtypeStruct((1, rows), F32), j...  70.6 us

profile of v4, /device:TPU:1, one launch (start us, length us, event | category | flops | bytes accessed | tf_op | source)
XLA Modules:
  0.0 74.0 jit_solution(8449450288417217680)
XLA Ops:
  1.9 70.6 %shard_map.103 = (f32[1,128]{1,0:T(1,128)}, f32[12,768]{1,0:T(8,128)}, f32[12,768]{1,0:T(8,128)}) custom-call(bf16[128,1536]{1,0:T(8,128)(2,1)} %picture_hbm.1, bf16[128,1536]{1,0:T(8,128)(2,1)} %caption_hbm.1, bf16[1536,768]{1,0:T(8,128)(2,1)} %picture_head_hbm.1, bf16[1536,768]{1,0:T(8,128)(2,1)} %caption_head_hbm.1, s32[1,128]{1,0:T(1,128)} %match_ref.1, ...), custom_call_target="tpu_custom_call" | custom-call | tf_op jit(solution)/shard_map/pallas_call | solution.py:366
  72.5 1.5 %shard_map.104 = (f32[1,128]{1,0:T(1,128)}, f32[12,768]{1,0:T(8,128)}, f32[12,768]{1,0:T(8,128)}) custom-call(f32[1,128]{1,0:T(1,128)} %get-tuple-element.9.loss_ref, f32[12,768]{1,0:T(8,128)} %get-tuple-element.10.image_ref, f32[12,768]{1,0:T(8,128)} %get-tuple-element.11.text_ref), custom_call_target="tpu_custom_call" | custom-call | tf_op jit(solution)/shard_map/pallas_call | solution.py:412

commit v5 on v4

--- a/solution.py
+++ b/solution.py
@@ -52,8 +52,8 @@
 
     loads = [
         pltpu.make_async_copy(caption_hbm, caption_ref, load.at[0]),
-        pltpu.make_async_copy(caption_head_hbm, caption_head, load.at[1]),
-        pltpu.make_async_copy(picture_hbm, picture_ref, load.at[2]),
+        pltpu.make_async_copy(picture_hbm, picture_ref, load.at[1]),
+        pltpu.make_async_copy(caption_head_hbm, caption_head, load.at[2]),
         pltpu.make_async_copy(picture_head_hbm, picture_head, load.at[3]),
     ]
     for copy_in in loads:
@@ -97,19 +97,45 @@
         sent.append(made)
         return at
 
+    def settle(count):
+        for made in sent[:count]:
+            made.wait_send()
+        del sent[:count]
+
     def landed(dst, at):
         pltpu.make_async_copy(dst, dst, recv.at[at]).wait()
 
+    loads[0].wait()
+    loads[1].wait()
     norm_at = []
     for t, tower_ref, head in ((0, caption_ref, caption_head), (1, picture_ref, picture_head)):
-        loads[2 * t].wait()
-        loads[2 * t + 1].wait()
+        loads[2 + t].wait()
         raw = jnp.dot(tower_ref[...], head[...], preferred_element_type=F32)
         raws[t] = raw
         norm_out[t] = as_row(jnp.sum(raw * raw, axis=1, keepdims=True))
         if t == 0:
             pl.semaphore_wait(barrier, len(greeted))
         norm_at.append(copy(norm_out.at[t], norm_in.at[t], peer))
+        if t == 0:
+            pair = jnp.concatenate([picture_ref[...], caption_ref[...]], axis=0)
+            lane = lax.broadcasted_iota(jnp.int32, (1, part), 1)
+            step = part // XS
+            section = sum(jnp.where(lane >= b * step, 1, 0) for b in range(1, XS))
+            for g in range(GROUP):
+                pick = order_ref[:, g * part : (g + 1) * part] - section * wide
+                chosen = lax.broadcasted_iota(jnp.int32, (wide, part), 0) == pick
+                one = jnp.where(chosen, 1.0, 0.0).astype(BF16)
+                acc = None
+                for b in range(XS):
+                    term = jnp.dot(pair[:, b * wide : (b + 1) * wide], one, preferred_element_type=F32)
+                    acc = term if acc is None else jnp.where(section == b, term, acc)
+                towers_out[g, 0] = acc[:rows].astype(BF16)
+                towers_out[g, 1] = acc[rows:].astype(BF16)
+            towers[mine] = towers_out[mine]
+            tower_at = copy(towers_out.at[y * 2 + 1 - core], towers.at[mine], sibling)
+            cross_at = used[0]
+            for c in range(2):
+                copy(towers_out.at[cross_slot + c], towers.at[mine], crossed[c], cross_at + core)
 
     def embedding(t):
         landed(norm_in.at[t], norm_at[t])
@@ -157,24 +183,6 @@
         "down": REACH - 1 - 2 * core,
         "outer": REACH - 3 + 6 * core,
     }
-
-    pair = jnp.concatenate([picture_ref[...], caption_ref[...]], axis=0)
-    for g in range(GROUP):
-        pick = order_ref[:, g * part : (g + 1) * part]
-        acc = None
-        for b in range(XS):
-            chosen = lax.broadcasted_iota(jnp.int32, (wide, part), 0) + b * wide == pick
-            one = jnp.where(chosen, 1.0, 0.0).astype(BF16)
-            term = jnp.dot(pair[:, b * wide : (b + 1) * wide], one, preferred_element_type=F32)
-            acc = term if acc is None else acc + term
-        towers_out[g, 0] = acc[:rows].astype(BF16)
-        towers_out[g, 1] = acc[rows:].astype(BF16)
-    towers[mine] = towers_out[mine]
-    tower_at = copy(towers_out.at[y * 2 + 1 - core], towers.at[mine], sibling)
-    cross_at = used[0]
-    for c in range(2):
-        copy(towers_out.at[cross_slot + c], towers.at[mine], crossed[c], cross_at + core)
-
 
     text_emb, text_inv = embedding(0)
     texts[REACH] = text_emb
@@ -271,6 +279,7 @@
         for h in range(2):
             back_at[t, h, "sibling"] = copy(backs.at[t, h, mine], backs.at[t, h, mine], sibling)
 
+    early = len(sent)
     spread_back(0, back)
     loss_out[...] = as_row(jnp.sum(loss_sum[...], axis=1, keepdims=True))[:1] * (1.0 / rows)
 
@@ -298,6 +307,7 @@
         down, images[...].reshape(MET * rows, half), FIRST, preferred_element_type=F32
     )
     spread_back(1, back_through(gradient, texts[REACH], as_column(text_dot), text_inv))
+    settle(early)
 
     far = cross_slot + core
     landed(towers.at[y * 2 + 1 - core], tower_at)
@@ -319,6 +329,7 @@
         x_out[t, h] = product.astype(BF16)
         for d in range(1, XS):
             x_at[t, h, d] = copy(x_out.at[t, h, lax.rem(x + d, XS)], x_in.at[t, h, d - 1], x_peers[d - 1])
+    settle(len(sent) - 2 * 2 * (XS - 1) // 2)
     z_at = {}
     for t, h in parts:
         value = total[t, h, x]
@@ -332,14 +343,14 @@
             z_out[t, h, c] = chunk.astype(BF16)
         for d in range(1, ZS):
             z_at[t, h, d] = copy(z_out.at[t, h, lax.rem(z + d, ZS)], z_in.at[t, h, d - 1], z_peers[d - 1])
+    settle(len(sent) - 4 * (ZS - 1))
     for t, h in parts:
         value = z_own[t, h, z]
         for d in range(1, ZS):
             landed(z_in.at[t, h, d - 1], z_at[t, h, d])
             value = value + z_in[t, h, d - 1].astype(F32)
         (image_out, text_out)[t][:, h * cut : (h + 1) * cut] = value[:12]
-    for made in sent:
-        made.wait_send()
+    settle(len(sent))
 
 
 def results(loss_ref, image_ref, text_ref, loss_out, image_out, text_out):

time: 74.3 us -> 73.7 us (level)
  Pallas kernels: 72 us -> 71.1 us
    pallas_call x1, Pallas kernels: 70.6 us -> 69.6 us  [shards(): pl.pallas_call(kernel, out_shape=[jax.ShapeDtypeStruct((1, rows), F32), j...]
where the time goes in v5:
time: 73.7 us; the launch traced here: 73 us
  Pallas kernels  71.1 us (96%)
  between operations  1.93 us (3%)
    pallas_call x1, Pallas kernels, shards(): pl.pallas_call(kernel, out_shape=[jax.ShapeDtypeStruct((1, rows), F32), j...  69.6 us

profile of v5, /device:TPU:1, one launch (start us, length us, event | category | flops | bytes accessed | tf_op | source)
XLA Modules:
  0.0 73.0 jit_solution(14339133595618629834)
XLA Ops:
  1.9 69.6 %shard_map.103 = (f32[1,128]{1,0:T(1,128)}, f32[12,768]{1,0:T(8,128)}, f32[12,768]{1,0:T(8,128)}) custom-call(bf16[128,1536]{1,0:T(8,128)(2,1)} %picture_hbm.1, bf16[128,1536]{1,0:T(8,128)(2,1)} %caption_hbm.1, bf16[1536,768]{1,0:T(8,128)(2,1)} %picture_head_hbm.1, bf16[1536,768]{1,0:T(8,128)(2,1)} %caption_head_hbm.1, s32[1,128]{1,0:T(1,128)} %match_ref.1, ...), custom_call_target="tpu_custom_call" | custom-call | tf_op jit(solution)/shard_map/pallas_call | solution.py:377
  71.6 1.5 %shard_map.104 = (f32[1,128]{1,0:T(1,128)}, f32[12,768]{1,0:T(8,128)}, f32[12,768]{1,0:T(8,128)}) custom-call(f32[1,128]{1,0:T(1,128)} %get-tuple-element.9.loss_ref, f32[12,768]{1,0:T(8,128)} %get-tuple-element.10.image_ref, f32[12,768]{1,0:T(8,128)} %get-tuple-element.11.text_ref), custom_call_target="tpu_custom_call" | custom-call | tf_op jit(solution)/shard_map/pallas_call | solution.py:423

commit v6 on v5

--- a/solution.py
+++ b/solution.py
@@ -142,21 +142,23 @@
         inverse = lax.rsqrt(as_column((norm_out[t] + norm_in[t])[:1]) + 1e-06)
         return (raws[t] * inverse).astype(BF16), inverse
 
-    size = rows // CHUNKS
+    def chunks(held):
+        return CHUNKS if held is texts else 1
 
     def piece(held, slot, c):
+        size = rows // chunks(held)
         return held.at[slot, pl.ds(c * size, size)]
 
     def spread_own(held):
         at = {}
-        for c in range(CHUNKS):
+        for c in range(chunks(held)):
             for by in (2, -2):
                 at[by, c] = copy(piece(held, REACH, c), piece(held, REACH - by, c), block(by))
         at["own"] = copy(held.at[REACH], held.at[REACH + 2 * core - 1], sibling)
         return at
 
     def relay(held, at):
-        for c in range(CHUNKS):
+        for c in range(chunks(held)):
             for by in (2, -2):
                 landed(piece(held, REACH - by, c), at[by, c])
                 at["on", by, c] = copy(piece(held, REACH - by, c), piece(held, REACH - 2 * by, c), block(by))
@@ -164,7 +166,7 @@
                 hand_over(held, at, name, by, c)
 
     def relayed(held, at):
-        for c in range(CHUNKS):
+        for c in range(chunks(held)):
             for by in (2, -2):
                 landed(piece(held, REACH - 2 * by, c), at["on", by, c])
             hand_over(held, at, "outer", outer, c)
@@ -173,7 +175,7 @@
         at[name, c] = copy(piece(held, REACH + by, c), piece(held, REACH + by - 1 + 2 * core, c), sibling)
 
     def handed(held, at, name):
-        for c in range(CHUNKS):
+        for c in range(chunks(held)):
             landed(piece(held, slot_of[name], c), at[name, c])
 
     outer = 4 - 8 * core

time: 73.7 us -> 73.8 us (level)
  no operation moved by 1% of the time
where the time goes in v6:
time: 73.8 us; the launch traced here: 73.6 us
  Pallas kernels  71.7 us (97%)
  between operations  1.93 us (3%)
    pallas_call x1, Pallas kernels, shards(): pl.pallas_call(kernel, out_shape=[jax.ShapeDtypeStruct((1, rows), F32), j...  70.2 us

profile of v6, /device:TPU:1, one launch (start us, length us, event | category | flops | bytes accessed | tf_op | source)
XLA Modules:
  0.0 73.6 jit_solution(9862425231200657231)
XLA Ops:
  1.9 70.2 %shard_map.103 = (f32[1,128]{1,0:T(1,128)}, f32[12,768]{1,0:T(8,128)}, f32[12,768]{1,0:T(8,128)}) custom-call(bf16[128,1536]{1,0:T(8,128)(2,1)} %picture_hbm.1, bf16[128,1536]{1,0:T(8,128)(2,1)} %caption_hbm.1, bf16[1536,768]{1,0:T(8,128)(2,1)} %picture_head_hbm.1, bf16[1536,768]{1,0:T(8,128)(2,1)} %caption_head_hbm.1, s32[1,128]{1,0:T(1,128)} %match_ref.1, ...), custom_call_target="tpu_custom_call" | custom-call | tf_op jit(solution)/shard_map/pallas_call | solution.py:379
  72.2 1.5 %shard_map.104 = (f32[1,128]{1,0:T(1,128)}, f32[12,768]{1,0:T(8,128)}, f32[12,768]{1,0:T(8,128)}) custom-call(f32[1,128]{1,0:T(1,128)} %get-tuple-element.9.loss_ref, f32[12,768]{1,0:T(8,128)} %get-tuple-element.10.image_ref, f32[12,768]{1,0:T(8,128)} %get-tuple-element.11.text_ref), custom_call_target="tpu_custom_call" | custom-call | tf_op jit(solution)/shard_map/pallas_call | solution.py:425
